TPU v7x, 1024 devices: a whole 8x8x8 slice. The times are simulated.
1024 devices in a mesh: gx: 32 (over y_lo, x, core), gy: 4 (over y_hi), gz: 8 (over z).
Axes of the slice: x: 8, y: 8 (y_hi: 4, y_lo: 2; y = y_hi * 2 + y_lo), z: 8, core: 2. Of those that a mesh axis runs over, the one named last changes fastest.
Arguments:
- source: float32 [32, 4, 8, 125, 256], P('gx', 'gy', 'gz'), may hold values from -6 to 6
- stiffness: float32 [125, 125], replicated
- relax: float32 [125], replicated, may hold values from 0.1 to 0.2
- owners: int32 [32, 4, 8, 256, 1], P('gx', 'gy', 'gz'), may hold values from 0 to 31; in each aligned block of 256 rows (0 to 255, 256 to 511, ..., all dimensions but the last counted through in order) at most 16 rows name the same one
- material: int32 [32, 4, 8, 256], P('gx', 'gy', 'gz'), may hold values from 0 to 1, as said below
Outputs:
- settled: float32 [32, 4, 8, 125, 512], P('gx', 'gy', 'gz')
- incoming: float32 [32, 4, 8, 6, 25, 256], P('gx', 'gy', 'gz')
Inputs may be any that keep to these rules, and one draw needn't show every extreme that they name: `owners`: within one subdomain no owner is named by more than 16 blocks, a bound that some block reaches in every draw. `material`: in each vertical column of blocks, the blocks below a seafloor depth drawn per column are elastic and those above are acoustic.
All inputs are finite; a program needn't handle non-finite values.
Results may differ from a plain program's by a relative error of at most 0.0001.
Values sent between devices are 32-bit elements; how exact they have to be, the bound alone decides.
A program may use at most 32 MiB of HBM per device.

v0:
```python
import jax
import jax.numpy as jnp
import numpy as np
from jax import lax
from jax.sharding import PartitionSpec as P

FACE = 25
SWEEPS_E = 8
SWEEPS_A = 2
ITERS = 2
BX = 4
BY = 8
BZ = 8


robin_gain = 1.0


def with_halo(block, sides, width):
    for axis, dim in sides:
        count = lax.axis_size(axis)
        forward = [(i, i + 1) for i in range(count - 1)]
        backward = [(target, source) for source, target in forward]
        low = lax.ppermute(
            lax.slice_in_dim(block, block.shape[dim] - width, None, axis=dim), axis, forward
        )
        high = lax.ppermute(lax.slice_in_dim(block, 0, width, axis=dim), axis, backward)
        block = jnp.concatenate([low, block, high], axis=dim)
    return block


def face_table():
    grid = np.arange(125).reshape(5, 5, 5)
    return np.stack(
        [
            grid[0].ravel(),
            grid[4].ravel(),
            grid[:, 0].ravel(),
            grid[:, 4].ravel(),
            grid[:, :, 0].ravel(),
            grid[:, :, 4].ravel(),
        ]
    )


def add_traces(field, traces, table):
    result = field
    for side in range(6):
        result = result.at[..., table[side], :].add(traces[..., side, :, :])
    return result


def relaxation(rhs, matf, stiffness, relax):
    scale = 1.0 + 2.0 * matf
    field = jnp.zeros_like(rhs)
    for sweep in range(SWEEPS_E):
        applied = jnp.dot(stiffness, field, precision=lax.Precision.HIGHEST)
        active = 1.0 if sweep < SWEEPS_A else matf
        field = field + active * (relax[:, None] * ((rhs - scale * applied) / scale))
    return field


def pass_traces(outgoing):
    count = outgoing.shape[2]
    grid = outgoing.reshape(6, FACE, BX, BY, BZ)
    padded = with_halo(grid, (("gx", 2), ("gy", 3), ("gz", 4)), 1)
    lower_x = padded[1, :, 0:BX, 1:-1, 1:-1]
    upper_x = padded[0, :, 2:, 1:-1, 1:-1]
    lower_y = padded[3, :, 1:-1, 0:BY, 1:-1]
    upper_y = padded[2, :, 1:-1, 2:, 1:-1]
    lower_z = padded[5, :, 1:-1, 1:-1, 0:BZ]
    upper_z = padded[4, :, 1:-1, 1:-1, 2:]
    stacked = jnp.stack([lower_x, upper_x, lower_y, upper_y, lower_z, upper_z])
    return stacked.reshape(6, FACE, count)


def shards(source, stiffness, relax, owners, material):
    table = face_table()
    highest = lax.Precision.HIGHEST
    field = source[0, 0, 0]
    count = field.shape[1]
    owner = owners[0, 0, 0, :, 0]
    matf = material[0, 0, 0].astype(jnp.float32)
    groups = lax.axis_size("gx")
    slots_each = 2 * count // groups
    onehot = (owner[:, None] == jnp.arange(groups, dtype=jnp.int32)[None, :]).astype(jnp.int32)
    rank = jnp.sum(jnp.cumsum(onehot, axis=0) * onehot, axis=1) - 1
    slot = owner * slots_each + rank
    packer = (slot[:, None] == jnp.arange(groups * slots_each, dtype=jnp.int32)[None, :]).astype(
        jnp.float32
    )
    unpacker = jnp.transpose(packer)
    mat_row = jnp.dot(matf[None, :], packer, precision=highest)
    incoming = jnp.zeros((6, FACE, count), jnp.float32)
    for step in range(ITERS):
        rhs = add_traces(field, incoming, table)
        sent = jnp.dot(rhs, packer, precision=highest)
        owned_rhs, owned_mat = (
            lax.all_to_all(sent, "gx", split_axis=1, concat_axis=1, tiled=True),
            lax.all_to_all(mat_row, "gx", split_axis=1, concat_axis=1, tiled=True),
        )
        owned_field = relaxation(owned_rhs, owned_mat, stiffness, relax)
        back = lax.all_to_all(owned_field, "gx", split_axis=1, concat_axis=1, tiled=True)
        home_field = jnp.dot(back, unpacker, precision=highest)
        outgoing = -incoming + 2.0 * robin_gain * home_field[table]
        incoming = pass_traces(outgoing)
    return (owned_field[None, None, None], incoming[None, None, None])


def solution(mesh):
    return jax.shard_map(
        shards,
        mesh=mesh,
        in_specs=(
            P("gx", "gy", "gz", None, None),
            P(),
            P(),
            P("gx", "gy", "gz", None, None),
            P("gx", "gy", "gz", None),
        ),
        out_specs=(P("gx", "gy", "gz", None, None), P("gx", "gy", "gz", None, None, None)),
        check_vma=False,
    )
```

profile of v0, /device:TPU:65, one launch (start us, length us, event | category | flops | bytes accessed | tf_op | source)
XLA Modules:
  0.0 195.2 jit_solution(16032252162110128623)
XLA Ops:
  3.7 2.4 %fusion.86 = f32[1,32,16]{2,0,1:T(1,128)} fusion(s32[32,16]{1,0:T(8,128)S(1)} %multiply_add_fusion, s32[256]{0:T(256)S(1)} %add_add_fusion, s32[1,1,1,256]{3,2,1,0:T(1,128)} %param.36), kind=kOutput, calls=%fused_computation.116 | convolution fusion | flops 1704192 | bytes 6144 | tf_op jit(solution)/shard_map/dot_general | solution.py:93
  6.0 7.8 %all-to-all-start.1 = ((f32[1,32,16]{2,0,1:T(1,128)}), f32[1,32,16]{2,0,1:T(1,128)S(1)}, u32[]{:S(2)}, u32[]{:S(2)}) async-start(f32[1,32,16]{2,0,1:T(1,128)} %fusion.86), calls=%async_computation.1 | async-start | bytes 32768 | tf_op jit(solution)/shard_map/all_to_all | solution.py:100
  13.9 0.9 copy.82
  15.6 0.9 scatter_custom_fusion.1
  16.6 0.9 scatter_custom_fusion.2
  17.5 0.9 scatter_custom_fusion.3
  18.5 0.8 scatter_custom_fusion.4
  20.1 1.4 fusion.85
  21.6 8.2 %all-to-all-start = ((f32[125,32,16]{0,2,1:T(8,128)}), f32[125,32,16]{0,2,1:T(8,128)S(1)}, u32[]{:S(2)}, u32[]{:S(2)}) async-start(f32[125,32,16]{0,2,1:T(8,128)} %bitcast.3), calls=%async_computation | async-start | bytes 524288 | tf_op jit(solution)/shard_map/all_to_all | solution.py:99
  31.3 10.5 %all-to-all-done = f32[125,32,16]{0,2,1:T(8,128)S(1)} async-done(((f32[125,32,16]{0,2,1:T(8,128)}), f32[125,32,16]{0,2,1:T(8,128)S(1)}, u32[]{:S(2)}, u32[]{:S(2)}) %all-to-all-start) | async-done | bytes 256032 | tf_op jit(solution)/shard_map/all_to_all | solution.py:99
  44.3 1.1 fusion.61
  45.4 5.0 %all-to-all-start.2 = ((f32[125,32,16]{0,2,1:T(8,128)}), f32[125,32,16]{0,2,1:T(8,128)S(1)}, u32[]{:S(2)}, u32[]{:S(2)}) async-start(f32[125,32,16]{0,2,1:T(8,128)} %bitcast.16), calls=%async_computation.2 | async-start | bytes 524288 | tf_op jit(solution)/shard_map/all_to_all | solution.py:103
  50.5 12.0 %all-to-all-done.2 = f32[125,32,16]{0,2,1:T(8,128)S(1)} async-done(((f32[125,32,16]{0,2,1:T(8,128)}), f32[125,32,16]{0,2,1:T(8,128)S(1)}, u32[]{:S(2)}, u32[]{:S(2)}) %all-to-all-start.2) | async-done | bytes 256032 | tf_op jit(solution)/shard_map/all_to_all | solution.py:103
  64.3 3.8 %collective-permute-start = (f32[6,25,1,8,8]{1,0,4,3,2:T(8,128)S(1)}, f32[6,25,1,8,8]{1,0,4,3,2:T(8,128)S(1)}, u32[]{:S(2)}, u32[]{:S(2)}) collective-permute-start(f32[6,25,1,8,8]{1,0,4,3,2:T(8,128)S(1)} %get-tuple-element.33), channel_id=1, source_target_pairs={{0,32},{32,64},{64,96},{96,128},{128,160},{160,192},{192,224},{224... | collective-permute-start | bytes 115208 | tf_op jit(solution)/shard_map/ppermute | solution.py:24
  68.0 1.9 collective-permute-start.1
  70.0 1.4 collective-permute-done
  71.4 4.3 %collective-permute-done.1 = f32[6,25,1,8,8]{1,0,4,3,2:T(8,128)S(1)} collective-permute-done((f32[6,25,1,8,8]{1,0,4,3,2:T(8,128)S(1)}, f32[6,25,1,8,8]{1,0,4,3,2:T(8,128)S(1)}, u32[]{:S(2)}, u32[]{:S(2)}) %collective-permute-start.1) | collective-permute-done | bytes 38432 | tf_op jit(solution)/shard_map/ppermute | solution.py:27
  75.8 2.6 %collective-permute-start.3 = (f32[6,25,6,1,8]{1,0,4,3,2:T(8,128)S(1)}, f32[6,25,6,1,8]{1,0,4,3,2:T(8,128)S(1)}, u32[]{:S(2)}, u32[]{:S(2)}) collective-permute-start(f32[6,25,6,1,8]{1,0,4,3,2:T(8,128)S(1)} %get-tuple-element.23), channel_id=1, source_target_pairs={{8,0},{16,8},{24,16},{9,1},{17,9},{25,17},{10,2},{18,10},{26,18},{... | collective-permute-start | bytes 86408 | tf_op jit(solution)/shard_map/ppermute | solution.py:27
  78.4 3.6 %collective-permute-start.2 = (f32[6,25,6,1,8]{1,0,4,3,2:T(8,128)S(1)}, f32[6,25,6,1,8]{1,0,4,3,2:T(8,128)S(1)}, u32[]{:S(2)}, u32[]{:S(2)}) collective-permute-start(f32[6,25,6,1,8]{1,0,4,3,2:T(8,128)S(1)} %get-tuple-element.24), channel_id=1, source_target_pairs={{0,8},{8,16},{16,24},{1,9},{9,17},{17,25},{2,10},{10,18},{18,26},{... | collective-permute-start | bytes 86408 | tf_op jit(solution)/shard_map/ppermute | solution.py:24
  82.0 5.5 %collective-permute-done.3 = f32[6,25,6,1,8]{1,0,4,3,2:T(8,128)S(1)} collective-permute-done((f32[6,25,6,1,8]{1,0,4,3,2:T(8,128)S(1)}, f32[6,25,6,1,8]{1,0,4,3,2:T(8,128)S(1)}, u32[]{:S(2)}, u32[]{:S(2)}) %collective-permute-start.3) | collective-permute-done | bytes 28832 | tf_op jit(solution)/shard_map/ppermute | solution.py:27
  87.5 5.0 %collective-permute-done.2 = f32[6,25,6,1,8]{1,0,4,3,2:T(8,128)S(1)} collective-permute-done((f32[6,25,6,1,8]{1,0,4,3,2:T(8,128)S(1)}, f32[6,25,6,1,8]{1,0,4,3,2:T(8,128)S(1)}, u32[]{:S(2)}, u32[]{:S(2)}) %collective-permute-start.2) | collective-permute-done | bytes 28832 | tf_op jit(solution)/shard_map/ppermute | solution.py:24
  92.5 0.8 pad_maximum_fusion.5
  93.3 1.4 collective-permute-start.5
  94.8 4.7 %collective-permute-start.4 = (f32[6,25,6,10,1]{1,0,4,3,2:T(8,128)}, f32[6,25,6,10,1]{1,0,4,3,2:T(8,128)}, u32[]{:S(2)}, u32[]{:S(2)}) collective-permute-start(f32[6,25,6,10,1]{1,0,4,3,2:T(8,128)} %get-tuple-element.17), channel_id=1, source_target_pairs={{0,1},{1,2},{2,3},{3,4},{4,5},{5,6},{6,7},{8,9},{9,10},{10,11},{11... | collective-permute-start | bytes 108008 | tf_op jit(solution)/shard_map/ppermute | solution.py:24
  99.9 0.8 scatter_fusion
  102.2 1.6 pad_maximum_fusion.29
  104.2 0.8 scatter_fusion.2
  106.7 1.0 scatter_fusion.5
  108.4 22.8 %all_to_all.58 = f32[125,32,16]{0,2,1:T(8,128)S(1)} all-to-all(f32[125,32,16]{0,2,1:T(8,128)S(1)} %bitcast.253), channel_id=1, replica_groups=mesh['gx'=32,'gy'=4,'gz'=8] {'gx'}, dimensions={1} | all-to-all | bytes 512000 | tf_op jit(solution)/shard_map/all_to_all | solution.py:99
  133.7 1.1 fusion.81
  134.8 5.0 %all-to-all-start.4 = ((f32[125,32,16]{0,2,1:T(8,128)}), f32[125,32,16]{0,2,1:T(8,128)S(1)}, u32[]{:S(2)}, u32[]{:S(2)}) async-start(f32[125,32,16]{0,2,1:T(8,128)} %bitcast.34), calls=%async_computation.4 | async-start | bytes 524288 | tf_op jit(solution)/shard_map/all_to_all | solution.py:103
  139.8 1.2 stack.6
  141.1 10.8 %all-to-all-done.4 = f32[125,32,16]{0,2,1:T(8,128)S(1)} async-done(((f32[125,32,16]{0,2,1:T(8,128)}), f32[125,32,16]{0,2,1:T(8,128)S(1)}, u32[]{:S(2)}, u32[]{:S(2)}) %all-to-all-start.4) | async-done | bytes 256032 | tf_op jit(solution)/shard_map/all_to_all | solution.py:103
  153.8 3.4 %collective-permute-start.7 = (f32[6,25,1,8,8]{1,0,4,3,2:T(8,128)S(1)}, f32[6,25,1,8,8]{1,0,4,3,2:T(8,128)S(1)}, u32[]{:S(2)}, u32[]{:S(2)}) collective-permute-start(f32[6,25,1,8,8]{1,0,4,3,2:T(8,128)S(1)} %get-tuple-element.28), channel_id=1, source_target_pairs={{32,0},{64,32},{96,64},{128,96},{160,128},{192,160},{224,192},{256... | collective-permute-start | bytes 115208 | tf_op jit(solution)/shard_map/ppermute | solution.py:27
  157.3 2.3 %collective-permute-start.6 = (f32[6,25,1,8,8]{1,0,4,3,2:T(8,128)S(1)}, f32[6,25,1,8,8]{1,0,4,3,2:T(8,128)S(1)}, u32[]{:S(2)}, u32[]{:S(2)}) collective-permute-start(f32[6,25,1,8,8]{1,0,4,3,2:T(8,128)S(1)} %get-tuple-element.29), channel_id=1, source_target_pairs={{0,32},{32,64},{64,96},{96,128},{128,160},{160,192},{192,224},{224... | collective-permute-start | bytes 115208 | tf_op jit(solution)/shard_map/ppermute | solution.py:24
  159.5 2.1 %collective-permute-done.7 = f32[6,25,1,8,8]{1,0,4,3,2:T(8,128)S(1)} collective-permute-done((f32[6,25,1,8,8]{1,0,4,3,2:T(8,128)S(1)}, f32[6,25,1,8,8]{1,0,4,3,2:T(8,128)S(1)}, u32[]{:S(2)}, u32[]{:S(2)}) %collective-permute-start.7) | collective-permute-done | bytes 38432 | tf_op jit(solution)/shard_map/ppermute | solution.py:27
  161.7 1.2 collective-permute-done.6
  162.9 4.1 %collective-permute-start.9 = (f32[6,25,6,1,8]{1,0,4,3,2:T(8,128)S(1)}, f32[6,25,6,1,8]{1,0,4,3,2:T(8,128)S(1)}, u32[]{:S(2)}, u32[]{:S(2)}) collective-permute-start(f32[6,25,6,1,8]{1,0,4,3,2:T(8,128)S(1)} %get-tuple-element.21), channel_id=1, source_target_pairs={{8,0},{16,8},{24,16},{9,1},{17,9},{25,17},{10,2},{18,10},{26,18},{... | collective-permute-start | bytes 86408 | tf_op jit(solution)/shard_map/ppermute | solution.py:27
  167.0 2.1 %collective-permute-start.8 = (f32[6,25,6,1,8]{1,0,4,3,2:T(8,128)S(1)}, f32[6,25,6,1,8]{1,0,4,3,2:T(8,128)S(1)}, u32[]{:S(2)}, u32[]{:S(2)}) collective-permute-start(f32[6,25,6,1,8]{1,0,4,3,2:T(8,128)S(1)} %get-tuple-element.22), channel_id=1, source_target_pairs={{0,8},{8,16},{16,24},{1,9},{9,17},{17,25},{2,10},{10,18},{18,26},{... | collective-permute-start | bytes 86408 | tf_op jit(solution)/shard_map/ppermute | solution.py:24
  169.1 1.8 copy.71
  170.9 4.4 %collective-permute-done.9 = f32[6,25,6,1,8]{1,0,4,3,2:T(8,128)S(1)} collective-permute-done((f32[6,25,6,1,8]{1,0,4,3,2:T(8,128)S(1)}, f32[6,25,6,1,8]{1,0,4,3,2:T(8,128)S(1)}, u32[]{:S(2)}, u32[]{:S(2)}) %collective-permute-start.9) | collective-permute-done | bytes 28832 | tf_op jit(solution)/shard_map/ppermute | solution.py:27
  175.3 5.3 %collective-permute-done.8 = f32[6,25,6,1,8]{1,0,4,3,2:T(8,128)S(1)} collective-permute-done((f32[6,25,6,1,8]{1,0,4,3,2:T(8,128)S(1)}, f32[6,25,6,1,8]{1,0,4,3,2:T(8,128)S(1)}, u32[]{:S(2)}, u32[]{:S(2)}) %collective-permute-start.8) | collective-permute-done | bytes 28832 | tf_op jit(solution)/shard_map/ppermute | solution.py:24
  180.7 1.3 collective-permute-start.11
  182.0 4.8 %collective-permute-start.10 = (f32[6,25,6,10,1]{1,0,4,3,2:T(8,128)S(1)}, f32[6,25,6,10,1]{1,0,4,3,2:T(8,128)S(1)}, u32[]{:S(2)}, u32[]{:S(2)}) collective-permute-start(f32[6,25,6,10,1]{1,0,4,3,2:T(8,128)S(1)} %get-tuple-element.13), channel_id=1, source_target_pairs={{0,1},{1,2},{2,3},{3,4},{4,5},{5,6},{6,7},{8,9},{9,10},{10,11},{11... | collective-permute-start | bytes 108008 | tf_op jit(solution)/shard_map/ppermute | solution.py:24
  187.0 3.6 %collective-permute-done.11 = f32[6,25,6,10,1]{1,0,4,3,2:T(8,128)S(1)} collective-permute-done((f32[6,25,6,10,1]{1,0,4,3,2:T(8,128)S(1)}, f32[6,25,6,10,1]{1,0,4,3,2:T(8,128)S(1)}, u32[]{:S(2)}, u32[]{:S(2)}) %collective-permute-start.11) | collective-permute-done | bytes 36032 | tf_op jit(solution)/shard_map/ppermute | solution.py:27
  190.5 1.8 collective-permute-done.10
  193.0 1.2 stack.7
  194.3 1.0 copy.72
  (81 shorter events, 20.5 us)
Async XLA Ops:
  0.6 18.7 %copy-start.2 = (s32[25]{0:T(128)S(1)}, s32[25]{0:T(128)}, u32[]{:S(2)}) copy-start(s32[25]{0:T(128)} %constant.61) | copy-start | bytes 304
  0.6 29.2 %copy-start = (f32[125,125]{1,0:T(8,128)S(1)}, f32[125,125]{1,0:T(8,128)}, u32[]{:S(2)}) copy-start(f32[125,125]{1,0:T(8,128)} %param.33) | copy-start | bytes 187504
  0.7 41.1 %copy-start.6 = (f32[125]{0:T(128)S(1)}, f32[125]{0:T(128)}, u32[]{:S(2)}) copy-start(f32[125]{0:T(128)} %param.34) | copy-start | bytes 1504
  6.0 15.6 %all-to-all-start.1 = ((f32[1,32,16]{2,0,1:T(1,128)}), f32[1,32,16]{2,0,1:T(1,128)S(1)}, u32[]{:S(2)}, u32[]{:S(2)}) async-start(f32[1,32,16]{2,0,1:T(1,128)} %fusion.86), calls=%async_computation.1 | async-start | bytes 32768 | tf_op jit(solution)/shard_map/all_to_all | solution.py:100
  21.6 20.1 %all-to-all-start = ((f32[125,32,16]{0,2,1:T(8,128)}), f32[125,32,16]{0,2,1:T(8,128)S(1)}, u32[]{:S(2)}, u32[]{:S(2)}) async-start(f32[125,32,16]{0,2,1:T(8,128)} %bitcast.3), calls=%async_computation | async-start | bytes 524288 | tf_op jit(solution)/shard_map/all_to_all | solution.py:99
  43.9 6.6 %copy-start.1 = (s32[150]{0:T(256)S(1)}, s32[150]{0:T(256)}, u32[]{:S(2)}) copy-start(s32[150]{0:T(256)} %constant.62) | copy-start | bytes 1804
  45.4 17.1 %all-to-all-start.2 = ((f32[125,32,16]{0,2,1:T(8,128)}), f32[125,32,16]{0,2,1:T(8,128)S(1)}, u32[]{:S(2)}, u32[]{:S(2)}) async-start(f32[125,32,16]{0,2,1:T(8,128)} %bitcast.16), calls=%async_computation.2 | async-start | bytes 524288 | tf_op jit(solution)/shard_map/all_to_all | solution.py:103
  64.3 7.1 %collective-permute-start = (f32[6,25,1,8,8]{1,0,4,3,2:T(8,128)S(1)}, f32[6,25,1,8,8]{1,0,4,3,2:T(8,128)S(1)}, u32[]{:S(2)}, u32[]{:S(2)}) collective-permute-start(f32[6,25,1,8,8]{1,0,4,3,2:T(8,128)S(1)} %get-tuple-element.33), channel_id=1, source_target_pairs={{0,32},{32,64},{64,96},{96,128},{128,160},{160,192},{192,224},{224... | collective-permute-start | bytes 115208 | tf_op jit(solution)/shard_map/ppermute | solution.py:24
  68.0 7.7 %collective-permute-start.1 = (f32[6,25,1,8,8]{1,0,4,3,2:T(8,128)S(1)}, f32[6,25,1,8,8]{1,0,4,3,2:T(8,128)S(1)}, u32[]{:S(2)}, u32[]{:S(2)}) collective-permute-start(f32[6,25,1,8,8]{1,0,4,3,2:T(8,128)S(1)} %get-tuple-element.32), channel_id=1, source_target_pairs={{32,0},{64,32},{96,64},{128,96},{160,128},{192,160},{224,192},{256... | collective-permute-start | bytes 115208 | tf_op jit(solution)/shard_map/ppermute | solution.py:27
  75.8 11.7 %collective-permute-start.3 = (f32[6,25,6,1,8]{1,0,4,3,2:T(8,128)S(1)}, f32[6,25,6,1,8]{1,0,4,3,2:T(8,128)S(1)}, u32[]{:S(2)}, u32[]{:S(2)}) collective-permute-start(f32[6,25,6,1,8]{1,0,4,3,2:T(8,128)S(1)} %get-tuple-element.23), channel_id=1, source_target_pairs={{8,0},{16,8},{24,16},{9,1},{17,9},{25,17},{10,2},{18,10},{26,18},{... | collective-permute-start | bytes 86408 | tf_op jit(solution)/shard_map/ppermute | solution.py:27
  78.4 14.1 %collective-permute-start.2 = (f32[6,25,6,1,8]{1,0,4,3,2:T(8,128)S(1)}, f32[6,25,6,1,8]{1,0,4,3,2:T(8,128)S(1)}, u32[]{:S(2)}, u32[]{:S(2)}) collective-permute-start(f32[6,25,6,1,8]{1,0,4,3,2:T(8,128)S(1)} %get-tuple-element.24), channel_id=1, source_target_pairs={{0,8},{8,16},{16,24},{1,9},{9,17},{17,25},{2,10},{10,18},{18,26},{... | collective-permute-start | bytes 86408 | tf_op jit(solution)/shard_map/ppermute | solution.py:24
  93.3 7.4 %copy-start.5 = (s32[25]{0:T(128)S(1)}, s32[25]{0:T(128)}, u32[]{:S(2)}) copy-start(s32[25]{0:T(128)} %constant.58) | copy-start | bytes 304
  93.3 8.2 %collective-permute-start.5 = (f32[6,25,6,10,1]{1,0,4,3,2:T(8,128)}, f32[6,25,6,10,1]{1,0,4,3,2:T(8,128)}, u32[]{:S(2)}, u32[]{:S(2)}) collective-permute-start(f32[6,25,6,10,1]{1,0,4,3,2:T(8,128)} %get-tuple-element.16), channel_id=1, source_target_pairs={{1,0},{2,1},{3,2},{4,3},{5,4},{6,5},{7,6},{9,8},{10,9},{11,10},{12... | collective-permute-start | bytes 108008 | tf_op jit(solution)/shard_map/ppermute | solution.py:27
  94.8 7.4 %collective-permute-start.4 = (f32[6,25,6,10,1]{1,0,4,3,2:T(8,128)}, f32[6,25,6,10,1]{1,0,4,3,2:T(8,128)}, u32[]{:S(2)}, u32[]{:S(2)}) collective-permute-start(f32[6,25,6,10,1]{1,0,4,3,2:T(8,128)} %get-tuple-element.17), channel_id=1, source_target_pairs={{0,1},{1,2},{2,3},{3,4},{4,5},{5,6},{6,7},{8,9},{9,10},{10,11},{11... | collective-permute-start | bytes 108008 | tf_op jit(solution)/shard_map/ppermute | solution.py:24
  101.6 2.6 %copy-start.4 = (s32[25]{0:T(128)S(1)}, s32[25]{0:T(128)}, u32[]{:S(2)}) copy-start(s32[25]{0:T(128)} %constant.59) | copy-start | bytes 304
  101.6 3.4 %copy-start.3 = (s32[25]{0:T(128)S(1)}, s32[25]{0:T(128)}, u32[]{:S(2)}) copy-start(s32[25]{0:T(128)} %constant.60) | copy-start | bytes 304
  134.8 17.1 %all-to-all-start.4 = ((f32[125,32,16]{0,2,1:T(8,128)}), f32[125,32,16]{0,2,1:T(8,128)S(1)}, u32[]{:S(2)}, u32[]{:S(2)}) async-start(f32[125,32,16]{0,2,1:T(8,128)} %bitcast.34), calls=%async_computation.4 | async-start | bytes 524288 | tf_op jit(solution)/shard_map/all_to_all | solution.py:103
  153.8 7.8 %collective-permute-start.7 = (f32[6,25,1,8,8]{1,0,4,3,2:T(8,128)S(1)}, f32[6,25,1,8,8]{1,0,4,3,2:T(8,128)S(1)}, u32[]{:S(2)}, u32[]{:S(2)}) collective-permute-start(f32[6,25,1,8,8]{1,0,4,3,2:T(8,128)S(1)} %get-tuple-element.28), channel_id=1, source_target_pairs={{32,0},{64,32},{96,64},{128,96},{160,128},{192,160},{224,192},{256... | collective-permute-start | bytes 115208 | tf_op jit(solution)/shard_map/ppermute | solution.py:27
  157.3 5.6 %collective-permute-start.6 = (f32[6,25,1,8,8]{1,0,4,3,2:T(8,128)S(1)}, f32[6,25,1,8,8]{1,0,4,3,2:T(8,128)S(1)}, u32[]{:S(2)}, u32[]{:S(2)}) collective-permute-start(f32[6,25,1,8,8]{1,0,4,3,2:T(8,128)S(1)} %get-tuple-element.29), channel_id=1, source_target_pairs={{0,32},{32,64},{64,96},{96,128},{128,160},{160,192},{192,224},{224... | collective-permute-start | bytes 115208 | tf_op jit(solution)/shard_map/ppermute | solution.py:24
  162.9 12.4 %collective-permute-start.9 = (f32[6,25,6,1,8]{1,0,4,3,2:T(8,128)S(1)}, f32[6,25,6,1,8]{1,0,4,3,2:T(8,128)S(1)}, u32[]{:S(2)}, u32[]{:S(2)}) collective-permute-start(f32[6,25,6,1,8]{1,0,4,3,2:T(8,128)S(1)} %get-tuple-element.21), channel_id=1, source_target_pairs={{8,0},{16,8},{24,16},{9,1},{17,9},{25,17},{10,2},{18,10},{26,18},{... | collective-permute-start | bytes 86408 | tf_op jit(solution)/shard_map/ppermute | solution.py:27
  167.0 13.6 %collective-permute-start.8 = (f32[6,25,6,1,8]{1,0,4,3,2:T(8,128)S(1)}, f32[6,25,6,1,8]{1,0,4,3,2:T(8,128)S(1)}, u32[]{:S(2)}, u32[]{:S(2)}) collective-permute-start(f32[6,25,6,1,8]{1,0,4,3,2:T(8,128)S(1)} %get-tuple-element.22), channel_id=1, source_target_pairs={{0,8},{8,16},{16,24},{1,9},{9,17},{17,25},{2,10},{10,18},{18,26},{... | collective-permute-start | bytes 86408 | tf_op jit(solution)/shard_map/ppermute | solution.py:24
  180.7 9.9 %collective-permute-start.11 = (f32[6,25,6,10,1]{1,0,4,3,2:T(8,128)S(1)}, f32[6,25,6,10,1]{1,0,4,3,2:T(8,128)S(1)}, u32[]{:S(2)}, u32[]{:S(2)}) collective-permute-start(f32[6,25,6,10,1]{1,0,4,3,2:T(8,128)S(1)} %get-tuple-element.12), channel_id=1, source_target_pairs={{1,0},{2,1},{3,2},{4,3},{5,4},{6,5},{7,6},{9,8},{10,9},{11,10},{12... | collective-permute-start | bytes 108008 | tf_op jit(solution)/shard_map/ppermute | solution.py:27
  182.0 10.4 %collective-permute-start.10 = (f32[6,25,6,10,1]{1,0,4,3,2:T(8,128)S(1)}, f32[6,25,6,10,1]{1,0,4,3,2:T(8,128)S(1)}, u32[]{:S(2)}, u32[]{:S(2)}) collective-permute-start(f32[6,25,6,10,1]{1,0,4,3,2:T(8,128)S(1)} %get-tuple-element.13), channel_id=1, source_target_pairs={{0,1},{1,2},{2,3},{3,4},{4,5},{5,6},{6,7},{8,9},{9,10},{10,11},{11... | collective-permute-start | bytes 108008 | tf_op jit(solution)/shard_map/ppermute | solution.py:24
where the time goes:
time: 196 us; the launch traced here: 195 us
  waiting for transfers between devices  68.5 us (35%)
  starting transfers between devices  61.9 us (32%)
  blocking collectives  22.8 us (12%)
  other arithmetic  17.9 us (9%)
  matrix products  12.6 us (6%)
  local copies, waits for them, and re-layouts  10.2 us (5%)
    all_to_all x1, blocking collectives, shards(): lax.all_to_all(sent, 'gx', split_axis=1, concat_axis=1, tiled=True)  22.8 us
    all_to_all x2, waiting for transfers between devices, shards(): lax.all_to_all(owned_field, 'gx', split_axis=1, concat_axis=1, tiled=True)  22.8 us
    ppermute x6, starting transfers between devices, with_halo(): lax.ppermute(lax.slice_in_dim(block, block.shape[dim] - width, None, axis...  21.1 us
    ppermute x6, waiting for transfers between devices, with_halo(): lax.ppermute(lax.slice_in_dim(block, 0, width, axis=dim), axis, backward)  19.8 us
    ppermute x6, waiting for transfers between devices, with_halo(): lax.ppermute(lax.slice_in_dim(block, block.shape[dim] - width, None, axis...  15.3 us
    ppermute x6, starting transfers between devices, with_halo(): lax.ppermute(lax.slice_in_dim(block, 0, width, axis=dim), axis, backward)  14.7 us
    all_to_all x1, waiting for transfers between devices, shards(): lax.all_to_all(sent, 'gx', split_axis=1, concat_axis=1, tiled=True)  10.5 us
    scatter-add x12, other arithmetic, add_traces(): result = result.at[..., table[side], :].add(traces[..., side, :, :])  10.3 us
  transfers between devices with their start and end apart: 16, of which 15 were waited for; matrix products, arithmetic and copies ran while one was open for 7% of the time, Pallas kernels for 0%

commit v1 on v0

v1 whole, which is shorter than its diff:
```python
import functools

import jax
import jax.numpy as jnp
from jax import lax
from jax.experimental import pallas as pl
from jax.experimental.pallas import tpu as pltpu
from jax.sharding import PartitionSpec as P

NODES = 125
FACE = 25
LANES = 128
COUNT = 256
SLOTS = 512
CAP = 16
GROUPS = 32
FACE_ROWS = 32
STACK = 6 * FACE_ROWS
MESH = pl.DeviceIdType.MESH
F32 = jnp.float32
BF16 = jnp.bfloat16
HIGHEST = lax.Precision.HIGHEST

HALO = ((0, 16), (16, 16), (32, 8), (40, 8), (48, 8), (56, 8))
HALO_ROWS = 64
ORDER = tuple(
    dy * 16 + dx * 2 + dc
    for dx in (4, 3, 5, 2, 6, 1, 7, 0)
    for dy in (1, 0)
    for dc in (1, 0)
    if dy + dx + dc
)


def iota(shape, dim):
    return lax.broadcasted_iota(jnp.int32, shape, dim)


def matmul(left, right):
    return lax.dot_general(
        left, right, (((1,), (0,)), ((), ())), preferred_element_type=F32
    )


def matmul_t(left, right):
    return lax.dot_general(
        left, right, (((1,), (1,)), ((), ())), preferred_element_type=F32
    )


def full(left, right):
    return lax.dot_general(
        left, right, (((1,), (0,)), ((), ())), precision=HIGHEST, preferred_element_type=F32
    )


def halves(values):
    high = values.astype(BF16)
    return high, (values - high.astype(F32)).astype(BF16)


def roll(values, shift):
    shift = shift % LANES
    return pltpu.roll(values, shift, 1) if shift else values


def face_rows():
    m = iota((FACE_ROWS, LANES), 0)
    node = iota((FACE_ROWS, LANES), 1)
    a = sum((m >= cut).astype(jnp.int32) for cut in (5, 10, 15, 20))
    b = m - 5 * a
    picks = (m, m + 100, 25 * a + b, 25 * a + b + 20, 5 * m, 5 * m + 4)
    faces = [jnp.where((node == pick) & (m < FACE), 1.0, 0.0) for pick in picks]
    return jnp.concatenate(faces, axis=0).astype(BF16)


def pieces(face):
    return [(r, t, face[8 * r : 8 * r + 8, LANES * t : LANES * t + LANES]) for r in range(4) for t in range(2)]


def total(terms):
    while len(terms) > 1:
        terms = [sum(terms[i : i + 2]) for i in range(0, len(terms), 2)]
    return terms[0]


def pack_halo(out, tx):
    lane = iota((8, LANES), 1)
    z, y = lane & 7, (lane >> 3) & 7
    low = lane < 64
    face = lambda f: out[FACE_ROWS * f : FACE_ROWS * (f + 1)]
    piece = {f: {(r, t): v for r, t, v in pieces(face(f))} for f in range(6)}
    for j in range(2):
        tx[8 * j : 8 * j + 8] = jnp.where(low, roll(piece[1][2 * j, 1], 64), piece[1][2 * j + 1, 1])
        tx[16 + 8 * j : 24 + 8 * j] = jnp.where(low, piece[0][2 * j, 0], roll(piece[0][2 * j + 1, 0], 64))

    def gather(f, keep, shift):
        return total([
            roll(jnp.where(keep, piece[f][r, t], 0.0), shift(2 * r + t)) for r in range(4) for t in range(2)
        ])

    tx[32:40] = gather(3, y == 7, lambda q: 8 * q - 56)
    tx[40:48] = gather(2, y == 0, lambda q: 8 * q)
    tx[48:56] = gather(5, z == 7, lambda q: q - 7)
    tx[56:64] = gather(4, z == 0, lambda q: q)


def shift_inside(out, inc):
    lane = iota((FACE_ROWS, LANES), 1)
    z, y = lane & 7, (lane >> 3) & 7
    low = lane < 64
    tile = lambda f, t: out[FACE_ROWS * f : FACE_ROWS * (f + 1), LANES * t : LANES * (t + 1)]

    def put(f, t, values):
        inc[t, FACE_ROWS * f : FACE_ROWS * (f + 1)] = values

    a, b = roll(tile(1, 0), 64), roll(tile(1, 1), 64)
    put(0, 0, jnp.where(low, 0.0, a))
    put(0, 1, jnp.where(low, a, b))
    a, b = roll(tile(0, 0), 64), roll(tile(0, 1), 64)
    put(1, 0, jnp.where(low, a, b))
    put(1, 1, jnp.where(low, b, 0.0))
    for t in range(2):
        put(2, t, jnp.where(y == 0, 0.0, roll(tile(3, t), 8)))
        put(3, t, jnp.where(y == 7, 0.0, roll(tile(2, t), -8)))
        put(4, t, jnp.where(z == 0, 0.0, roll(tile(5, t), 1)))
        put(5, t, jnp.where(z == 7, 0.0, roll(tile(4, t), -1)))


def add_halo(rx, inc, inner):
    lane = iota((8, LANES), 1)
    z, y = lane & 7, (lane >> 3) & 7
    low = lane < 64
    has = [jnp.full((8, LANES), flag, jnp.int32) > 0 for flag in inner]

    def add(f, r, t, keep, values):
        rows = slice(FACE_ROWS * f + 8 * r, FACE_ROWS * f + 8 * r + 8)
        inc[t, rows] = jnp.where(keep, values, inc[t, rows])

    for j in range(2):
        part = rx[8 * j : 8 * j + 8]
        add(0, 2 * j, 0, low & has[0], part)
        add(0, 2 * j + 1, 0, low & has[0], roll(part, 64))
        part = rx[16 + 8 * j : 24 + 8 * j]
        add(1, 2 * j, 1, (lane >= 64) & has[1], roll(part, 64))
        add(1, 2 * j + 1, 1, (lane >= 64) & has[1], part)
    for r in range(4):
        for t in range(2):
            q = 2 * r + t
            add(2, r, t, (y == 0) & has[2], roll(rx[32:40], -8 * q))
            add(3, r, t, (y == 7) & has[3], roll(rx[40:48], 56 - 8 * q))
            add(4, r, t, (z == 0) & has[4], roll(rx[48:56], -q))
            add(5, r, t, (z == 7) & has[5], roll(rx[56:64], 7 - q))


def kernel(
    source_hbm, stiffness_hbm, relax_hbm, owners_hbm, material_hbm,
    settled_hbm, incoming_hbm,
    src, stiff, relax, owner, mat, kpad, rpad, packer, moved, landed, turned, tx, rx, inc,
    in_sem, out_sem, halo_send, halo_recv, move_send, move_recv,
):
    gx, gy, gz = (lax.axis_index(axis) for axis in ("gx", "gy", "gz"))
    loads = [
        pltpu.make_async_copy(stiffness_hbm, stiff, in_sem.at[0]),
        pltpu.make_async_copy(relax_hbm, relax, in_sem.at[1]),
        pltpu.make_async_copy(source_hbm.at[:, 0, pl.ds(0, LANES)], src.at[0, pl.ds(0, NODES)], in_sem.at[2]),
        pltpu.make_async_copy(source_hbm.at[:, 0, pl.ds(LANES, LANES)], src.at[1, pl.ds(0, NODES)], in_sem.at[5]),
        pltpu.make_async_copy(owners_hbm, owner, in_sem.at[3]),
        pltpu.make_async_copy(material_hbm, mat, in_sem.at[4]),
    ]
    for t in range(2):
        src[t, 120:128] = jnp.zeros((8, LANES), F32)
    for load in loads:
        load.start()

    my_y, my_x, my_c = gx // 16, (gx // 2) % 8, gx % 2

    def peer(chunk):
        dy, dx, dc = chunk // 16, (chunk // 2) % 8, chunk % 2
        return ((my_y + dy) % 2) * 16 + ((my_x + dx) % 8) * 2 + (my_c + dc) % 2

    barrier = pltpu.get_barrier_semaphore()
    for chunk in ORDER:
        pl.semaphore_signal(barrier, 1, device_id=(peer(chunk), gy, gz), device_id_type=MESH)
    sides = (
        ((gx + 1) % 32, gy, gz), ((gx + 31) % 32, gy, gz),
        (gx, (gy + 1) % 4, gz), (gx, (gy + 3) % 4, gz),
        (gx, gy, (gz + 1) % 8), (gx, gy, (gz + 7) % 8),
    )
    for side in sides[2:]:
        pl.semaphore_signal(barrier, 1, device_id=side, device_id_type=MESH)
    inner = (gx, 31 - gx, gy, 3 - gy, gz, 7 - gz)

    kpad[...] = jnp.zeros((LANES, LANES), F32)
    rpad[...] = jnp.zeros((8, LANES), F32)
    loads[0].wait()
    loads[1].wait()
    kpad[0:NODES, 0:NODES] = stiff[...]
    rpad[0:1, 0:NODES] = relax[...]
    eye = iota((LANES, LANES), 0) == iota((LANES, LANES), 1)
    row = jnp.broadcast_to(rpad[0:1], (LANES, LANES))
    diag = jnp.where(eye, row, 0.0)
    col = jnp.sum(diag, axis=1, keepdims=True)
    scaled = col * kpad[...]
    step = jnp.where(eye, 1.0, 0.0) - scaled
    sum2 = 2.0 * diag - scaled * row
    step2 = full(step, step)
    sum4 = sum2 + full(step2, sum2)
    step4 = full(step2, step2)
    sum8 = sum4 + full(step4, sum4)
    elastic_op, acoustic_op = sum8 * (1.0 / 3.0), sum2

    for load in loads[2:]:
        load.wait()
    elastic = jnp.broadcast_to(mat[...], (LANES, COUNT)) > 0
    source = jnp.concatenate([src[0], src[1]], axis=1)
    field = jnp.where(elastic, full(elastic_op, source), full(acoustic_op, source))
    pick = face_rows()
    high, low = halves(field)
    faces = matmul(pick, high) + matmul(pick, low)
    out = 2.0 * faces
    pack_halo(out, tx.at[0])

    def halo_copies(step):
        return [
            pltpu.make_async_remote_copy(
                src_ref=tx.at[step, pl.ds(at, rows)],
                dst_ref=rx.at[step, pl.ds(at, rows)],
                send_sem=halo_send.at[step, i],
                recv_sem=halo_recv.at[step, i],
                device_id=sides[i],
                device_id_type=MESH,
            )
            for i, (at, rows) in enumerate(HALO)
        ]

    pl.semaphore_wait(barrier, len(ORDER) + 4)
    first = halo_copies(0)
    for copy in first:
        copy.start()

    shift_inside(out, inc)
    ops = []
    for op in (elastic_op, acoustic_op):
        high, low = halves(op)
        nodes = matmul_t(high, pick) + matmul_t(low, pick)
        high, low = halves(nodes)
        ops.append((high, low))
    on_nodes = [jnp.concatenate([ops[0][i], ops[1][i]], axis=0) for i in range(2)]
    on_faces = [
        jnp.concatenate([matmul(pick, ops[0][i]), matmul(pick, ops[1][i])], axis=0).astype(BF16) for i in range(2)
    ]

    names = owner[...]
    named = iota((GROUPS, COUNT), 0) == jnp.broadcast_to(names, (GROUPS, COUNT))
    before = jnp.where(iota((COUNT, COUNT), 0) < iota((COUNT, COUNT), 1), 1.0, 0.0).astype(BF16)
    counts = matmul(jnp.where(named, 1.0, 0.0).astype(BF16), before)
    rank = jnp.sum(jnp.where(named, counts, 0.0), axis=0, keepdims=True).astype(jnp.int32)
    chunk = (
        (((names >> 4) ^ my_y) << 4)
        | ((((names >> 1) - my_x) & 7) << 1)
        | ((names & 1) ^ my_c)
    )
    slot = chunk * CAP + rank
    for k in range(4):
        here = iota((LANES, COUNT), 0) + k * LANES == jnp.broadcast_to(slot, (LANES, COUNT))
        packer[k * LANES : (k + 1) * LANES] = jnp.where(here, 1.0, 0.0).astype(BF16)

    for copy in first:
        copy.wait_recv()
    add_halo(rx.at[0], inc, inner)

    incoming = jnp.concatenate([inc[0], inc[1]], axis=1)
    high, low = halves(incoming)

    def on_traces(op):
        return matmul(op[0], high) + matmul(op[0], low) + matmul(op[1], high)

    change = on_traces(on_nodes)
    field = field + jnp.where(elastic, change[0:LANES], change[LANES : 2 * LANES])
    both = jnp.concatenate(halves(field), axis=0)
    for k in range(4):
        part = matmul_t(packer[k * LANES : (k + 1) * LANES], both)
        moved[k * LANES : (k + 1) * LANES] = part[:, 0:LANES] + part[:, LANES : 2 * LANES]
    moves = []
    for chunk in ORDER:
        copy = pltpu.make_async_remote_copy(
            src_ref=moved.at[pl.ds(chunk * CAP, CAP)],
            dst_ref=landed.at[pl.ds(pl.multiple_of(gx * CAP, CAP), CAP)],
            send_sem=move_send.at[chunk],
            recv_sem=move_recv.at[chunk],
            device_id=(peer(chunk), gy, gz),
            device_id_type=MESH,
        )
        copy.start()
        moves.append(copy)
    landed[pl.ds(pl.multiple_of(gx * CAP, CAP), CAP)] = moved[0:CAP]

    change = on_traces(on_faces)
    face_elastic = jnp.broadcast_to(mat[...], (STACK, COUNT)) > 0
    faces = faces + jnp.where(face_elastic, change[0:STACK], change[STACK : 2 * STACK])
    out = 2.0 * faces - incoming
    pack_halo(out, tx.at[1])
    second = halo_copies(1)
    for copy in second:
        copy.start()
    shift_inside(out, inc)
    for copy in second:
        copy.wait_recv()
    add_halo(rx.at[1], inc, inner)
    results = []
    for f in range(6):
        for t in range(2):
            results.append(
                pltpu.make_async_copy(
                    inc.at[t, pl.ds(f * FACE_ROWS, FACE)],
                    incoming_hbm.at[f, :, 0, pl.ds(t * LANES, LANES)],
                    out_sem.at[2 * f + t],
                )
            )
            results[-1].start()

    for copy in moves:
        copy.wait_recv()
    for k in range(4):
        turned[k] = landed[k * LANES : (k + 1) * LANES].T
        results.append(
            pltpu.make_async_copy(
                turned.at[k, pl.ds(0, NODES)], settled_hbm.at[:, 0, pl.ds(k * LANES, LANES)], out_sem.at[12 + k]
            )
        )
        results[-1].start()
    for copy in first + second + moves:
        copy.wait_send()
    for copy in results:
        copy.wait()


def shards(source, stiffness, relax, owners, material):
    anywhere = pl.BlockSpec(memory_space=pl.ANY)
    settled, incoming = pl.pallas_call(
        kernel,
        out_shape=(
            jax.ShapeDtypeStruct((NODES, 1, SLOTS), F32),
            jax.ShapeDtypeStruct((6, FACE, 1, COUNT), F32),
        ),
        in_specs=[anywhere] * 5,
        out_specs=(anywhere, anywhere),
        scratch_shapes=[
            pltpu.VMEM((2, LANES, LANES), F32),
            pltpu.VMEM((NODES, NODES), F32),
            pltpu.VMEM((1, NODES), F32),
            pltpu.VMEM((1, COUNT), jnp.int32),
            pltpu.VMEM((1, COUNT), jnp.int32),
            pltpu.VMEM((LANES, LANES), F32),
            pltpu.VMEM((8, LANES), F32),
            pltpu.VMEM((SLOTS, COUNT), BF16),
            pltpu.VMEM((SLOTS, LANES), F32),
            pltpu.VMEM((SLOTS, LANES), F32),
            pltpu.VMEM((4, LANES, LANES), F32),
            pltpu.VMEM((2, HALO_ROWS, LANES), F32),
            pltpu.VMEM((2, HALO_ROWS, LANES), F32),
            pltpu.VMEM((2, STACK, LANES), F32),
            pltpu.SemaphoreType.DMA((6,)),
            pltpu.SemaphoreType.DMA((16,)),
            pltpu.SemaphoreType.DMA((2, 6)),
            pltpu.SemaphoreType.DMA((2, 6)),
            pltpu.SemaphoreType.DMA((GROUPS,)),
            pltpu.SemaphoreType.DMA((GROUPS,)),
        ],
        compiler_params=pltpu.CompilerParams(
            collective_id=0, has_side_effects=True, vmem_limit_bytes=48 * 1024 * 1024
        ),
    )(
        source.reshape(NODES, 1, COUNT),
        stiffness,
        relax.reshape(1, NODES),
        owners.reshape(1, COUNT),
        material.reshape(1, COUNT),
    )
    return (
        settled.reshape(1, 1, 1, NODES, SLOTS),
        incoming.reshape(1, 1, 1, 6, FACE, COUNT),
    )


def solution(mesh):
    return jax.shard_map(
        shards,
        mesh=mesh,
        in_specs=(
            P("gx", "gy", "gz", None, None),
            P(),
            P(),
            P("gx", "gy", "gz", None, None),
            P("gx", "gy", "gz", None),
        ),
        out_specs=(P("gx", "gy", "gz", None, None), P("gx", "gy", "gz", None, None, None)),
        check_vma=False,
    )
```

time: 196 us -> 39.8 us (0.20)
  the two profiles are of different devices: /device:TPU:65 before, /device:TPU:1 now
where the time goes in v1:
time: 39.8 us; the launch traced here: 39.6 us
  Pallas kernels  35.2 us (88%)
  local copies, waits for them, and re-layouts  3.78 us (9%)
  between operations  0.67 us (2%)
    pallas_call x1, Pallas kernels, shards(): pl.pallas_call(kernel, out_shape=(jax.ShapeDtypeStruct((NODES, 1, SLOTS),...  35.2 us
    unnamed x12, local copies, waits for them, and re-layouts  3.78 us

profile of v1, /device:TPU:1, one launch (start us, length us, event | category | flops | bytes accessed | tf_op | source)
XLA Modules:
  0.0 39.6 jit_solution(6974526764368613637)
XLA Ops:
  0.6 0.0 copy-start.3
  0.6 0.0 copy-start.2
  0.7 0.0 copy-start.4
  0.7 0.7 %copy-done.3 = s32[1,1,1,256]{3,2,1,0:T(1,128)S(1)} copy-done((s32[1,1,1,256]{3,2,1,0:T(1,128)S(1)}, s32[1,1,1,256]{3,2,1,0:T(1,128)}, u32[]{:S(2)}) %copy-start.3) | copy-done | bytes 1048
  1.3 0.0 copy-done.2
  1.3 0.0 copy-done.4
  1.3 0.0 copy-start
  1.3 0.9 %copy-done = f32[1,1,1,125,256]{4,2,3,1,0:T(1,128)S(1)} copy-done((f32[1,1,1,125,256]{4,2,3,1,0:T(1,128)S(1)}, f32[1,1,1,125,256]{4,2,3,1,0:T(1,128)}, u32[]{:S(2)}) %copy-start) | copy-done | bytes 128024
  2.2 0.0 copy-start.1
  2.2 0.8 %copy-done.1 = f32[125,125]{1,0:T(8,128)S(1)} copy-done((f32[125,125]{1,0:T(8,128)S(1)}, f32[125,125]{1,0:T(8,128)}, u32[]{:S(2)}) %copy-start.1) | copy-done | bytes 62524
  3.1 35.2 %shard_map.68 = (f32[125,1,512]{2,1,0:T(1,128)S(1)}, f32[6,25,1,256]{3,2,1,0:T(1,128)S(1)}) custom-call(f32[125,1,256]{2,1,0:T(1,128)S(1)} %bitcast.12, f32[125,125]{1,0:T(8,128)S(1)} %copy-done.1, f32[1,125]{1,0:T(1,128)S(1)} %bitcast.15, s32[1,256]{1,0:T(1,128)S(1)} %bitcast.13, s32[1,256]{1,0:T(1,128)S(1)} %bitcast.14), custom_call_target="tpu_custom_call" | custom-call | tf_op jit(solution)/shard_map/pallas_call | solution.py:341
  38.2 0.7 %copy.11 = f32[1,1,1,125,512]{4,2,3,1,0:T(1,128)} copy(f32[1,1,1,125,512]{4,2,3,1,0:T(1,128)S(1)} %bitcast.10) | data formatting | bytes 512000
  38.9 0.7 %copy.12 = f32[1,1,1,6,25,256]{5,2,4,3,1,0:T(1,128)} copy(f32[1,1,1,6,25,256]{5,2,4,3,1,0:T(1,128)S(1)} %bitcast.11) | data formatting | bytes 307200
Async XLA Ops:
  0.6 0.7 %copy-start.3 = (s32[1,1,1,256]{3,2,1,0:T(1,128)S(1)}, s32[1,1,1,256]{3,2,1,0:T(1,128)}, u32[]{:S(2)}) copy-start(s32[1,1,1,256]{3,2,1,0:T(1,128)} %param.9) | copy-start | bytes 3076
  0.6 0.7 %copy-start.2 = (s32[1,1,1,256,1]{3,4,2,1,0:T(1,128)S(1)}, s32[1,1,1,256,1]{3,4,2,1,0:T(1,128)}, u32[]{:S(2)}) copy-start(s32[1,1,1,256,1]{3,4,2,1,0:T(1,128)} %param.8) | copy-start | bytes 3076
  0.7 0.7 %copy-start.4 = (f32[125]{0:T(128)S(1)}, f32[125]{0:T(128)}, u32[]{:S(2)}) copy-start(f32[125]{0:T(128)} %param.7) | copy-start | bytes 1504
  1.3 0.9 %copy-start = (f32[1,1,1,125,256]{4,2,3,1,0:T(1,128)S(1)}, f32[1,1,1,125,256]{4,2,3,1,0:T(1,128)}, u32[]{:S(2)}) copy-start(f32[1,1,1,125,256]{4,2,3,1,0:T(1,128)} %param.5) | copy-start | bytes 384004
  2.2 0.8 %copy-start.1 = (f32[125,125]{1,0:T(8,128)S(1)}, f32[125,125]{1,0:T(8,128)}, u32[]{:S(2)}) copy-start(f32[125,125]{1,0:T(8,128)} %stiffness_hbm.1) | copy-start | bytes 187504

commit v2 on v1

--- a/solution.py
+++ b/solution.py
@@ -25,8 +25,8 @@
 HALO_ROWS = 64
 ORDER = tuple(
     dy * 16 + dx * 2 + dc
-    for dx in (4, 3, 5, 2, 6, 1, 7, 0)
-    for dy in (1, 0)
+    for dx in (0, 1, 7, 2, 6, 3, 5, 4)
+    for dy in (0, 1)
     for dc in (1, 0)
     if dy + dx + dc
 )
@@ -131,7 +131,7 @@
     lane = iota((8, LANES), 1)
     z, y = lane & 7, (lane >> 3) & 7
     low = lane < 64
-    has = [jnp.full((8, LANES), flag, jnp.int32) > 0 for flag in inner]
+    has = [jnp.full((8, LANES), inner[i ^ 1].astype(jnp.int32), jnp.int32) > 0 for i in range(6)]
 
     def add(f, r, t, keep, values):
         rows = slice(FACE_ROWS * f + 8 * r, FACE_ROWS * f + 8 * r + 8)
@@ -155,9 +155,9 @@
 
 def kernel(
     source_hbm, stiffness_hbm, relax_hbm, owners_hbm, material_hbm,
-    settled_hbm, incoming_hbm,
-    src, stiff, relax, owner, mat, kpad, rpad, packer, moved, landed, turned, tx, rx, inc,
-    in_sem, out_sem, halo_send, halo_recv, move_send, move_recv,
+    landed, inc,
+    src, stiff, relax, owner, mat, kpad, rpad, packer, moved, tx, rx,
+    in_sem, halo_send, halo_recv, move_send, move_recv,
 ):
     gx, gy, gz = (lax.axis_index(axis) for axis in ("gx", "gy", "gz"))
     loads = [
@@ -172,6 +172,7 @@
         src[t, 120:128] = jnp.zeros((8, LANES), F32)
     for load in loads:
         load.start()
+    rx[...] = jnp.zeros_like(rx)
 
     my_y, my_x, my_c = gx // 16, (gx // 2) % 8, gx % 2
 
@@ -179,17 +180,30 @@
         dy, dx, dc = chunk // 16, (chunk // 2) % 8, chunk % 2
         return ((my_y + dy) % 2) * 16 + ((my_x + dx) % 8) * 2 + (my_c + dc) % 2
 
+    sides = (
+        (gx + 1, gy, gz), (gx - 1, gy, gz), (gx, gy + 1, gz), (gx, gy - 1, gz), (gx, gy, gz + 1), (gx, gy, gz - 1),
+    )
+    there = (gx < 31, gx > 0, gy < 3, gy > 0, gz < 7, gz > 0)
+    around = sum(flag.astype(jnp.int32) for flag in there[2:])
     barrier = pltpu.get_barrier_semaphore()
-    for chunk in ORDER:
-        pl.semaphore_signal(barrier, 1, device_id=(peer(chunk), gy, gz), device_id_type=MESH)
-    sides = (
-        ((gx + 1) % 32, gy, gz), ((gx + 31) % 32, gy, gz),
-        (gx, (gy + 1) % 4, gz), (gx, (gy + 3) % 4, gz),
-        (gx, gy, (gz + 1) % 8), (gx, gy, (gz + 7) % 8),
-    )
-    for side in sides[2:]:
-        pl.semaphore_signal(barrier, 1, device_id=side, device_id_type=MESH)
-    inner = (gx, 31 - gx, gy, 3 - gy, gz, 7 - gz)
+
+    def greet(device):
+        pl.semaphore_signal(barrier, 1, device_id=device, device_id_type=MESH)
+
+    for i in range(2, 6):
+        pl.when(there[i])(functools.partial(greet, sides[i]))
+
+    @pl.when(gx == 0)
+    def _():
+        pl.semaphore_wait(barrier, GROUPS - 1 + around)
+        for chunk in ORDER:
+            greet((peer(chunk), gy, gz))
+
+    @pl.when(gx > 0)
+    def _():
+        for chunk in ORDER:
+            other = peer(chunk)
+            pl.when(other > 0)(functools.partial(greet, (other, gy, gz)))
 
     kpad[...] = jnp.zeros((LANES, LANES), F32)
     rpad[...] = jnp.zeros((8, LANES), F32)
@@ -221,23 +235,48 @@
     out = 2.0 * faces
     pack_halo(out, tx.at[0])
 
-    def halo_copies(step):
-        return [
-            pltpu.make_async_remote_copy(
-                src_ref=tx.at[step, pl.ds(at, rows)],
-                dst_ref=rx.at[step, pl.ds(at, rows)],
-                send_sem=halo_send.at[step, i],
-                recv_sem=halo_recv.at[step, i],
-                device_id=sides[i],
-                device_id_type=MESH,
-            )
-            for i, (at, rows) in enumerate(HALO)
-        ]
-
-    pl.semaphore_wait(barrier, len(ORDER) + 4)
-    first = halo_copies(0)
-    for copy in first:
-        copy.start()
+    def halo_copy(step, i):
+        at, rows = HALO[i]
+        return pltpu.make_async_remote_copy(
+            src_ref=tx.at[step, pl.ds(at, rows)],
+            dst_ref=rx.at[step, pl.ds(at, rows)],
+            send_sem=halo_send.at[step, i],
+            recv_sem=halo_recv.at[step, i],
+            device_id=sides[i],
+            device_id_type=MESH,
+        )
+
+    def halo_start(step, i, when):
+        @pl.when(when)
+        def _():
+            halo_copy(step, i).start()
+
+    def halo_wait_recv(step):
+        for i in range(6):
+            @pl.when(there[i ^ 1])
+            def _():
+                halo_copy(step, i).wait_recv()
+
+    def halo_wait_send(step):
+        for i in range(6):
+            @pl.when(there[i])
+            def _():
+                halo_copy(step, i).wait_send()
+
+    @pl.when(gx > 0)
+    def _():
+        pl.semaphore_wait(barrier, GROUPS - 2 + around)
+        greet((0, gy, gz))
+
+    halo_start(0, 0, there[0])
+    halo_start(0, 1, gx > 1)
+    for i in range(2, 6):
+        halo_start(0, i, there[i])
+
+    @pl.when(gx == 1)
+    def _():
+        pl.semaphore_wait(barrier, 1)
+        halo_copy(0, 1).start()
 
     shift_inside(out, inc)
     ops = []
@@ -266,9 +305,8 @@
         here = iota((LANES, COUNT), 0) + k * LANES == jnp.broadcast_to(slot, (LANES, COUNT))
         packer[k * LANES : (k + 1) * LANES] = jnp.where(here, 1.0, 0.0).astype(BF16)
 
-    for copy in first:
-        copy.wait_recv()
-    add_halo(rx.at[0], inc, inner)
+    halo_wait_recv(0)
+    add_halo(rx.at[0], inc, there)
 
     incoming = jnp.concatenate([inc[0], inc[1]], axis=1)
     high, low = halves(incoming)
@@ -276,38 +314,56 @@
     def on_traces(op):
         return matmul(op[0], high) + matmul(op[0], low) + matmul(op[1], high)
 
+    change = on_traces(on_faces)
+    face_elastic = jnp.broadcast_to(mat[...], (STACK, COUNT)) > 0
+    faces = faces + jnp.where(face_elastic, change[0:STACK], change[STACK : 2 * STACK])
+    out = 2.0 * faces - incoming
+    pack_halo(out, tx.at[1])
     change = on_traces(on_nodes)
     field = field + jnp.where(elastic, change[0:LANES], change[LANES : 2 * LANES])
     both = jnp.concatenate(halves(field), axis=0)
+    for i in range(6):
+        halo_start(1, i, there[i])
     for k in range(4):
         part = matmul_t(packer[k * LANES : (k + 1) * LANES], both)
         moved[k * LANES : (k + 1) * LANES] = part[:, 0:LANES] + part[:, LANES : 2 * LANES]
-    moves = []
-    for chunk in ORDER:
-        copy = pltpu.make_async_remote_copy(
-            src_ref=moved.at[pl.ds(chunk * CAP, CAP)],
-            dst_ref=landed.at[pl.ds(pl.multiple_of(gx * CAP, CAP), CAP)],
+
+    mine = pl.ds(pl.multiple_of(gx * CAP, CAP), CAP)
+
+    def move(chunk):
+        return pltpu.make_async_remote_copy(
+            src_ref=moved.at[pl.ds(pl.multiple_of(chunk * CAP, CAP), CAP)],
+            dst_ref=landed.at[mine],
             send_sem=move_send.at[chunk],
             recv_sem=move_recv.at[chunk],
             device_id=(peer(chunk), gy, gz),
             device_id_type=MESH,
         )
-        copy.start()
-        moves.append(copy)
-    landed[pl.ds(pl.multiple_of(gx * CAP, CAP), CAP)] = moved[0:CAP]
-
-    change = on_traces(on_faces)
-    face_elastic = jnp.broadcast_to(mat[...], (STACK, COUNT)) > 0
-    faces = faces + jnp.where(face_elastic, change[0:STACK], change[STACK : 2 * STACK])
-    out = 2.0 * faces - incoming
-    pack_halo(out, tx.at[1])
-    second = halo_copies(1)
-    for copy in second:
-        copy.start()
+
+    for chunk in ORDER:
+        pl.when(peer(chunk) > 0)(lambda chunk=chunk: move(chunk).start())
+
+    @pl.when(gx > 1)
+    def _():
+        pl.semaphore_wait(barrier, 1)
+
+    @pl.when(gx > 0)
+    def _():
+        move(my_y * 16 + ((8 - my_x) % 8) * 2 + my_c).start()
+
+    landed[mine] = moved[0:CAP]
     shift_inside(out, inc)
-    for copy in second:
-        copy.wait_recv()
-    add_halo(rx.at[1], inc, inner)
+    halo_wait_recv(1)
+    add_halo(rx.at[1], inc, there)
+    for chunk in ORDER:
+        move(chunk).wait_recv()
+    halo_wait_send(0)
+    halo_wait_send(1)
+    for chunk in ORDER:
+        move(chunk).wait_send()
+
+
+def finish(landed, inc, settled_hbm, incoming_hbm, turned, out_sem):
     results = []
     for f in range(6):
         for t in range(2):
@@ -319,9 +375,6 @@
                 )
             )
             results[-1].start()
-
-    for copy in moves:
-        copy.wait_recv()
     for k in range(4):
         turned[k] = landed[k * LANES : (k + 1) * LANES].T
         results.append(
@@ -330,22 +383,25 @@
             )
         )
         results[-1].start()
-    for copy in first + second + moves:
-        copy.wait_send()
     for copy in results:
         copy.wait()
 
 
 def shards(source, stiffness, relax, owners, material):
     anywhere = pl.BlockSpec(memory_space=pl.ANY)
-    settled, incoming = pl.pallas_call(
+    vmem = pl.BlockSpec(memory_space=pltpu.VMEM)
+    operands = (
+        source.reshape(NODES, 1, COUNT),
+        stiffness,
+        relax.reshape(1, NODES),
+        owners.reshape(1, COUNT),
+        material.reshape(1, COUNT),
+    )
+    landed, inc = pl.pallas_call(
         kernel,
-        out_shape=(
-            jax.ShapeDtypeStruct((NODES, 1, SLOTS), F32),
-            jax.ShapeDtypeStruct((6, FACE, 1, COUNT), F32),
-        ),
+        out_shape=(pltpu.VMEM((SLOTS, LANES), F32), pltpu.VMEM((2, STACK, LANES), F32)),
         in_specs=[anywhere] * 5,
-        out_specs=(anywhere, anywhere),
+        out_specs=(vmem, vmem),
         scratch_shapes=[
             pltpu.VMEM((2, LANES, LANES), F32),
             pltpu.VMEM((NODES, NODES), F32),
@@ -356,28 +412,26 @@
             pltpu.VMEM((8, LANES), F32),
             pltpu.VMEM((SLOTS, COUNT), BF16),
             pltpu.VMEM((SLOTS, LANES), F32),
-            pltpu.VMEM((SLOTS, LANES), F32),
-            pltpu.VMEM((4, LANES, LANES), F32),
             pltpu.VMEM((2, HALO_ROWS, LANES), F32),
             pltpu.VMEM((2, HALO_ROWS, LANES), F32),
-            pltpu.VMEM((2, STACK, LANES), F32),
             pltpu.SemaphoreType.DMA((6,)),
-            pltpu.SemaphoreType.DMA((16,)),
             pltpu.SemaphoreType.DMA((2, 6)),
             pltpu.SemaphoreType.DMA((2, 6)),
             pltpu.SemaphoreType.DMA((GROUPS,)),
             pltpu.SemaphoreType.DMA((GROUPS,)),
         ],
         compiler_params=pltpu.CompilerParams(
-            collective_id=0, has_side_effects=True, vmem_limit_bytes=48 * 1024 * 1024
+            collective_id=0, has_side_effects=True, vmem_limit_bytes=32 * 1024 * 1024
         ),
-    )(
-        source.reshape(NODES, 1, COUNT),
-        stiffness,
-        relax.reshape(1, NODES),
-        owners.reshape(1, COUNT),
-        material.reshape(1, COUNT),
-    )
+    )(*(pltpu.with_memory_space_constraint(x, pltpu.HBM) for x in operands))
+    settled, incoming = pl.pallas_call(
+        finish,
+        out_shape=(pltpu.HBM((NODES, 1, SLOTS), F32), pltpu.HBM((6, FACE, 1, COUNT), F32)),
+        in_specs=(vmem, vmem),
+        out_specs=(anywhere, anywhere),
+        scratch_shapes=[pltpu.VMEM((4, LANES, LANES), F32), pltpu.SemaphoreType.DMA((16,))],
+        compiler_params=pltpu.CompilerParams(vmem_limit_bytes=32 * 1024 * 1024),
+    )(landed, inc)
     return (
         settled.reshape(1, 1, 1, NODES, SLOTS),
         incoming.reshape(1, 1, 1, 6, FACE, COUNT),

time: 39.8 us -> 26.7 us (0.67)
  the two profiles are of different devices: /device:TPU:1 before, /device:TPU:160 now
where the time goes in v2:
time: 26.7 us; the launch traced here: 26.5 us
  Pallas kernels  25.8 us (97%)
  between operations  0.64 us (2%)
    pallas_call x1, Pallas kernels, shards(): pl.pallas_call(kernel, out_shape=(pltpu.VMEM((SLOTS, LANES), F32), pltpu....  24.9 us
    pallas_call x1, Pallas kernels, shards(): pl.pallas_call(finish, out_shape=(pltpu.HBM((NODES, 1, SLOTS), F32), pltp...  0.93 us

profile of v2, /device:TPU:160, one launch (start us, length us, event | category | flops | bytes accessed | tf_op | source)
XLA Modules:
  0.0 26.5 jit_solution(14591688793571598088)
XLA Ops:
  0.6 24.9 %shard_map.68 = (f32[512,128]{1,0:T(8,128)S(1)}, f32[2,192,128]{2,1,0:T(8,128)S(1)}) custom-call(f32[125,1,256]{2,1,0:T(1,128)} %bitcast.10, f32[125,125]{1,0:T(8,128)} %stiffness_hbm.1, f32[1,125]{1,0:T(1,128)} %bitcast.13, s32[1,256]{1,0:T(1,128)} %bitcast.11, s32[1,256]{1,0:T(1,128)} %bitcast.12), custom_call_target="tpu_custom_call" | custom-call | tf_op jit(solution)/shard_map/pallas_call | solution.py:400
  25.6 0.9 %shard_map.69 = (f32[125,1,512]{2,1,0:T(1,128)}, f32[6,25,1,256]{3,2,1,0:T(1,128)}) custom-call(f32[512,128]{1,0:T(8,128)S(1)} %get-tuple-element.6.landed, f32[2,192,128]{2,1,0:T(8,128)S(1)} %get-tuple-element.7.inc), custom_call_target="tpu_custom_call" | custom-call | tf_op jit(solution)/shard_map/pallas_call | solution.py:427

commit v3 on v2

--- a/solution.py
+++ b/solution.py
@@ -23,13 +23,8 @@
 
 HALO = ((0, 16), (16, 16), (32, 8), (40, 8), (48, 8), (56, 8))
 HALO_ROWS = 64
-ORDER = tuple(
-    dy * 16 + dx * 2 + dc
-    for dx in (0, 1, 7, 2, 6, 3, 5, 4)
-    for dy in (0, 1)
-    for dc in (1, 0)
-    if dy + dx + dc
-)
+DX = (4, 3, 5, 2, 6, 1, 7, 0)
+ORDER = range(GROUPS - 1)
 
 
 def iota(shape, dim):
@@ -157,7 +152,7 @@
     source_hbm, stiffness_hbm, relax_hbm, owners_hbm, material_hbm,
     landed, inc,
     src, stiff, relax, owner, mat, kpad, rpad, packer, moved, tx, rx,
-    in_sem, halo_send, halo_recv, move_send, move_recv,
+    in_sem, halo_send, halo_recv, move_send, move_recv, side_sem, ready_sem, first_sem, relay, relay_send, relay_recv,
 ):
     gx, gy, gz = (lax.axis_index(axis) for axis in ("gx", "gy", "gz"))
     loads = [
@@ -176,34 +171,78 @@
 
     my_y, my_x, my_c = gx // 16, (gx // 2) % 8, gx % 2
 
+    def number(flag):
+        return flag.astype(jnp.int32)
+
+    def peer_at(chunk):
+        dx, dy, dc = DX[chunk // 4], 1 - chunk // 2 % 2, 1 - chunk % 2
+        return (my_y + dy) % 2, (my_x + dx) % 8, (my_c + dc) % 2
+
     def peer(chunk):
-        dy, dx, dc = chunk // 16, (chunk // 2) % 8, chunk % 2
-        return ((my_y + dy) % 2) * 16 + ((my_x + dx) % 8) * 2 + (my_c + dc) % 2
+        y, x, c = peer_at(chunk)
+        return y * 16 + x * 2 + c
+
+    def rank_of(y, x, c):
+        return jnp.maximum(2 * jnp.minimum(x, 8 - x) - 1 + number(x > 4), 0) * 4 + y * 2 + 1 - c
+
+    def rank_at(index):
+        return rank_of(index // 16, (index // 2) % 8, index % 2)
+
+    line0 = (gy == 0) & (gz == 0)
+    last = line0 & (gx == 0)
+    rank = rank_of(my_y, my_x, my_c)
+    my_rank = rank + 32 * number(last)
+
+    def is_later(chunk):
+        y, x, c = peer_at(chunk)
+        return rank_of(y, x, c) + 32 * number(line0 & (y + x + c == 0)) > my_rank
+
+    earlier_peers = jnp.where(last, 31, rank - number(line0 & (rank > 1)))
+    later_peers = jnp.where(last, 0, 31 - number(line0) - earlier_peers)
 
     sides = (
         (gx + 1, gy, gz), (gx - 1, gy, gz), (gx, gy + 1, gz), (gx, gy - 1, gz), (gx, gy, gz + 1), (gx, gy, gz - 1),
     )
     there = (gx < 31, gx > 0, gy < 3, gy > 0, gz < 7, gz > 0)
-    around = sum(flag.astype(jnp.int32) for flag in there[2:])
+    no = gx < 0
+    to_last = (
+        no, (gx == 1) & line0, no, (gx == 0) & (gy == 1) & (gz == 0), no, (gx == 0) & (gy == 0) & (gz == 1),
+    )
+    usual = (rank_at(gx + 1) > rank, rank_at(gx - 1) > rank, gy < 2, gy == 3, gz >= 0, no)
+    later = [there[i] & (to_last[i] | (jnp.logical_not(last) & usual[i])) for i in range(6)]
+    earlier = [there[i] & jnp.logical_not(later[i]) for i in range(6)]
+    greeted = earlier_peers + sum(number(earlier[i]) for i in range(2, 6)) + number(to_last[3] | to_last[5])
+
+    def signal(semaphore, device):
+        pl.semaphore_signal(semaphore, 1, device_id=device, device_id_type=MESH)
+
     barrier = pltpu.get_barrier_semaphore()
-
-    def greet(device):
-        pl.semaphore_signal(barrier, 1, device_id=device, device_id_type=MESH)
-
     for i in range(2, 6):
-        pl.when(there[i])(functools.partial(greet, sides[i]))
-
-    @pl.when(gx == 0)
-    def _():
-        pl.semaphore_wait(barrier, GROUPS - 1 + around)
+        pl.when(later[i])(functools.partial(signal, barrier, sides[i]))
+
+    @pl.when(to_last[1])
+    def _():
+        signal(barrier, (0, 1, 0))
+        signal(barrier, (0, 0, 1))
+
+    @pl.when(jnp.logical_not(last))
+    def _():
         for chunk in ORDER:
-            greet((peer(chunk), gy, gz))
-
-    @pl.when(gx > 0)
-    def _():
+            pl.when(is_later(chunk))(functools.partial(signal, barrier, (peer(chunk), gy, gz)))
+
+    def answer_sides():
+        @pl.when(greeted > 0)
+        def _():
+            pl.semaphore_wait(barrier, greeted)
+
+        for i in range(6):
+            pl.when(earlier[i])(functools.partial(signal, side_sem.at[i ^ 1], sides[i]))
+
+    @pl.when(last)
+    def _():
+        answer_sides()
         for chunk in ORDER:
-            other = peer(chunk)
-            pl.when(other > 0)(functools.partial(greet, (other, gy, gz)))
+            signal(first_sem, (peer(chunk), gy, gz))
 
     kpad[...] = jnp.zeros((LANES, LANES), F32)
     rpad[...] = jnp.zeros((8, LANES), F32)
@@ -223,6 +262,7 @@
     step4 = full(step2, step2)
     sum8 = sum4 + full(step4, sum4)
     elastic_op, acoustic_op = sum8 * (1.0 / 3.0), sum2
+    pl.when(jnp.logical_not(last))(answer_sides)
 
     for load in loads[2:]:
         load.wait()
@@ -263,20 +303,49 @@
             def _():
                 halo_copy(step, i).wait_send()
 
-    @pl.when(gx > 0)
-    def _():
-        pl.semaphore_wait(barrier, GROUPS - 2 + around)
-        greet((0, gy, gz))
-
-    halo_start(0, 0, there[0])
-    halo_start(0, 1, gx > 1)
-    for i in range(2, 6):
-        halo_start(0, i, there[i])
-
-    @pl.when(gx == 1)
-    def _():
-        pl.semaphore_wait(barrier, 1)
-        halo_copy(0, 1).start()
+    for i in range(6):
+        halo_start(0, i, earlier[i])
+
+    @pl.when(jnp.logical_not(last))
+    def _():
+        for chunk in ORDER:
+            pl.when(jnp.logical_not(is_later(chunk)))(
+                functools.partial(signal, ready_sem, (peer(chunk), gy, gz))
+            )
+
+    def relay_in(i, k):
+        at, rows = HALO[i]
+        return pltpu.make_async_remote_copy(
+            src_ref=tx.at[0, pl.ds(at, rows)],
+            dst_ref=relay.at[pl.ds(8 * k, rows)],
+            send_sem=halo_send.at[0, i],
+            recv_sem=relay_recv.at[k],
+            device_id=(1, 0, 0),
+            device_id_type=MESH,
+        )
+
+    def relay_out(i, k):
+        at, rows = HALO[i]
+        return pltpu.make_async_remote_copy(
+            src_ref=relay.at[pl.ds(8 * k, rows)],
+            dst_ref=rx.at[0, pl.ds(at, rows)],
+            send_sem=relay_send.at[k],
+            recv_sem=halo_recv.at[0, i],
+            device_id=(0, 0, 0),
+            device_id_type=MESH,
+        )
+
+    for k, i in enumerate((3, 5)):
+        pl.when(to_last[i])(lambda k=k, i=i: relay_in(i, k).start())
+
+    def halo_start_later():
+        for i in range(6):
+            @pl.when(later[i] & jnp.logical_not(to_last[i]))
+            def _():
+                pl.semaphore_wait(side_sem.at[i], 1)
+                halo_copy(0, i).start()
+
+    halo_start_later()
 
     shift_inside(out, inc)
     ops = []
@@ -294,17 +363,24 @@
     named = iota((GROUPS, COUNT), 0) == jnp.broadcast_to(names, (GROUPS, COUNT))
     before = jnp.where(iota((COUNT, COUNT), 0) < iota((COUNT, COUNT), 1), 1.0, 0.0).astype(BF16)
     counts = matmul(jnp.where(named, 1.0, 0.0).astype(BF16), before)
-    rank = jnp.sum(jnp.where(named, counts, 0.0), axis=0, keepdims=True).astype(jnp.int32)
-    chunk = (
-        (((names >> 4) ^ my_y) << 4)
-        | ((((names >> 1) - my_x) & 7) << 1)
-        | ((names & 1) ^ my_c)
-    )
-    slot = chunk * CAP + rank
+    place = jnp.sum(jnp.where(named, counts, 0.0), axis=0, keepdims=True).astype(jnp.int32)
+    ahead = ((names >> 1) - my_x) & 7
+    near = jnp.minimum(ahead, 8 - ahead)
+    ring = jnp.maximum(7 - 2 * near + jnp.where(ahead > 4, 1, 0), 0)
+    chunk = 4 * ring + 2 * (1 - ((names >> 4) ^ my_y)) + 1 - ((names & 1) ^ my_c)
+    slot = chunk * CAP + place
     for k in range(4):
         here = iota((LANES, COUNT), 0) + k * LANES == jnp.broadcast_to(slot, (LANES, COUNT))
         packer[k * LANES : (k + 1) * LANES] = jnp.where(here, 1.0, 0.0).astype(BF16)
 
+    @pl.when(to_last[1])
+    def _():
+        pl.semaphore_wait(side_sem.at[1], 1)
+        halo_copy(0, 1).start()
+        for k, i in enumerate((3, 5)):
+            relay_in(i, k).wait_recv()
+            relay_out(i, k).start()
+
     halo_wait_recv(0)
     add_halo(rx.at[0], inc, there)
 
@@ -313,45 +389,52 @@
 
     def on_traces(op):
         return matmul(op[0], high) + matmul(op[0], low) + matmul(op[1], high)
+
+    change = on_traces(on_nodes)
+    field = field + jnp.where(elastic, change[0:LANES], change[LANES : 2 * LANES])
+    both = jnp.concatenate(halves(field), axis=0)
+    mine = pl.ds(pl.multiple_of(gx * CAP, CAP), CAP)
+
+    def move(chunk, device=None):
+        return pltpu.make_async_remote_copy(
+            src_ref=moved.at[pl.ds(pl.multiple_of(chunk * CAP, CAP), CAP)],
+            dst_ref=landed.at[mine],
+            send_sem=move_send.at[chunk],
+            recv_sem=move_recv.at[chunk],
+            device_id=device or (peer(chunk), gy, gz),
+            device_id_type=MESH,
+        )
+
+    @pl.when(later_peers > 0)
+    def _():
+        pl.semaphore_wait(ready_sem, later_peers)
+
+    for k in range(4):
+        part = matmul_t(packer[k * LANES : (k + 1) * LANES], both)
+        moved[k * LANES : (k + 1) * LANES] = part[:, 0:LANES] + part[:, LANES : 2 * LANES]
+        for chunk in ORDER[8 * k : 8 * k + 8]:
+            pl.when(jnp.logical_not(line0 & (peer(chunk) == 0)))(lambda chunk=chunk: move(chunk).start())
+    landed[mine] = moved[SLOTS - CAP : SLOTS]
 
     change = on_traces(on_faces)
     face_elastic = jnp.broadcast_to(mat[...], (STACK, COUNT)) > 0
     faces = faces + jnp.where(face_elastic, change[0:STACK], change[STACK : 2 * STACK])
     out = 2.0 * faces - incoming
     pack_halo(out, tx.at[1])
-    change = on_traces(on_nodes)
-    field = field + jnp.where(elastic, change[0:LANES], change[LANES : 2 * LANES])
-    both = jnp.concatenate(halves(field), axis=0)
+    for i in (3, 5):
+        @pl.when(to_last[i])
+        def _():
+            pl.semaphore_wait(side_sem.at[i], 1)
     for i in range(6):
         halo_start(1, i, there[i])
-    for k in range(4):
-        part = matmul_t(packer[k * LANES : (k + 1) * LANES], both)
-        moved[k * LANES : (k + 1) * LANES] = part[:, 0:LANES] + part[:, LANES : 2 * LANES]
-
-    mine = pl.ds(pl.multiple_of(gx * CAP, CAP), CAP)
-
-    def move(chunk):
-        return pltpu.make_async_remote_copy(
-            src_ref=moved.at[pl.ds(pl.multiple_of(chunk * CAP, CAP), CAP)],
-            dst_ref=landed.at[mine],
-            send_sem=move_send.at[chunk],
-            recv_sem=move_recv.at[chunk],
-            device_id=(peer(chunk), gy, gz),
-            device_id_type=MESH,
-        )
-
-    for chunk in ORDER:
-        pl.when(peer(chunk) > 0)(lambda chunk=chunk: move(chunk).start())
-
-    @pl.when(gx > 1)
-    def _():
-        pl.semaphore_wait(barrier, 1)
-
-    @pl.when(gx > 0)
-    def _():
-        move(my_y * 16 + ((8 - my_x) % 8) * 2 + my_c).start()
-
-    landed[mine] = moved[0:CAP]
+
+    @pl.when(line0 & (gx > 0))
+    def _():
+        pl.semaphore_wait(first_sem, 1)
+        ahead = (8 - my_x) % 8
+        ring = jnp.maximum(7 - 2 * jnp.minimum(ahead, 8 - ahead) + number(ahead > 4), 0)
+        move(4 * ring + 2 * (1 - my_y) + 1 - my_c, (0, gy, gz)).start()
+
     shift_inside(out, inc)
     halo_wait_recv(1)
     add_halo(rx.at[1], inc, there)
@@ -359,6 +442,12 @@
         move(chunk).wait_recv()
     halo_wait_send(0)
     halo_wait_send(1)
+
+    @pl.when(to_last[1])
+    def _():
+        for k, i in enumerate((3, 5)):
+            relay_out(i, k).wait_send()
+
     for chunk in ORDER:
         move(chunk).wait_send()
 
@@ -419,6 +508,12 @@
             pltpu.SemaphoreType.DMA((2, 6)),
             pltpu.SemaphoreType.DMA((GROUPS,)),
             pltpu.SemaphoreType.DMA((GROUPS,)),
+            pltpu.SemaphoreType.REGULAR((6,)),
+            pltpu.SemaphoreType.REGULAR,
+            pltpu.SemaphoreType.REGULAR,
+            pltpu.VMEM((16, LANES), F32),
+            pltpu.SemaphoreType.DMA((2,)),
+            pltpu.SemaphoreType.DMA((2,)),
         ],
         compiler_params=pltpu.CompilerParams(
             collective_id=0, has_side_effects=True, vmem_limit_bytes=32 * 1024 * 1024

time: 26.7 us -> 24.7 us (0.925)
  the two profiles are of different devices: /device:TPU:160 before, /device:TPU:1 now
where the time goes in v3:
time: 24.7 us; the launch traced here: 24.3 us
  Pallas kernels  23.7 us (96%)
  between operations  0.64 us (3%)
    pallas_call x1, Pallas kernels, shards(): pl.pallas_call(kernel, out_shape=(pltpu.VMEM((SLOTS, LANES), F32), pltpu....  22.7 us
    pallas_call x1, Pallas kernels, shards(): pl.pallas_call(finish, out_shape=(pltpu.HBM((NODES, 1, SLOTS), F32), pltp...  0.93 us

profile of v3, /device:TPU:1, one launch (start us, length us, event | category | flops | bytes accessed | tf_op | source)
XLA Modules:
  0.0 24.3 jit_solution(4979786019599036334)
XLA Ops:
  0.6 22.7 %shard_map.68 = (f32[512,128]{1,0:T(8,128)S(1)}, f32[2,192,128]{2,1,0:T(8,128)S(1)}) custom-call(f32[125,1,256]{2,1,0:T(1,128)} %bitcast.10, f32[125,125]{1,0:T(8,128)} %stiffness_hbm.1, f32[1,125]{1,0:T(1,128)} %bitcast.13, s32[1,256]{1,0:T(1,128)} %bitcast.11, s32[1,256]{1,0:T(1,128)} %bitcast.12), custom_call_target="tpu_custom_call" | custom-call | tf_op jit(solution)/shard_map/pallas_call | solution.py:489
  23.4 0.9 %shard_map.69 = (f32[125,1,512]{2,1,0:T(1,128)}, f32[6,25,1,256]{3,2,1,0:T(1,128)}) custom-call(f32[512,128]{1,0:T(8,128)S(1)} %get-tuple-element.6.landed, f32[2,192,128]{2,1,0:T(8,128)S(1)} %get-tuple-element.7.inc), custom_call_target="tpu_custom_call" | custom-call | tf_op jit(solution)/shard_map/pallas_call | solution.py:522

commit v4 on v3

--- a/solution.py
+++ b/solution.py
@@ -25,6 +25,7 @@
 HALO_ROWS = 64
 DX = (4, 3, 5, 2, 6, 1, 7, 0)
 ORDER = range(GROUPS - 1)
+LATE_ORDER = (20, 24, 21, 25, 22, 26, 23, 27, 30, 12, 16, 13, 17, 14, 18, 15, 19, 0, 8, 1, 9, 2, 10, 3, 11, 28, 29)
 
 
 def iota(shape, dim):
@@ -45,7 +46,7 @@
 
 def full(left, right):
     return lax.dot_general(
-        left, right, (((1,), (0,)), ((), ())), precision=HIGHEST, preferred_element_type=F32
+        left, right, (((1,), (0,)), ((), ())), precision=lax.Precision.HIGH, preferred_element_type=F32
     )
 
 
@@ -152,11 +153,14 @@
     source_hbm, stiffness_hbm, relax_hbm, owners_hbm, material_hbm,
     landed, inc,
     src, stiff, relax, owner, mat, kpad, rpad, packer, moved, tx, rx,
-    in_sem, halo_send, halo_recv, move_send, move_recv, side_sem, ready_sem, first_sem, relay, relay_send, relay_recv,
+    in_sem, halo_send, halo_recv, move_send, move_recv, side_sem, ready_sem, first_sem, relay, relay_send, relay_recv, nodes, picked,
 ):
     gx, gy, gz = (lax.axis_index(axis) for axis in ("gx", "gy", "gz"))
     loads = [
-        pltpu.make_async_copy(stiffness_hbm, stiff, in_sem.at[0]),
+        *(
+            pltpu.make_async_copy(stiffness_hbm.at[pl.ds(at, rows)], stiff.at[pl.ds(at, rows)], in_sem.at[6 + k])
+            for k, (at, rows) in enumerate(((0, 32), (32, 32), (64, 32), (96, 29)))
+        ),
         pltpu.make_async_copy(relax_hbm, relax, in_sem.at[1]),
         pltpu.make_async_copy(source_hbm.at[:, 0, pl.ds(0, LANES)], src.at[0, pl.ds(0, NODES)], in_sem.at[2]),
         pltpu.make_async_copy(source_hbm.at[:, 0, pl.ds(LANES, LANES)], src.at[1, pl.ds(0, NODES)], in_sem.at[5]),
@@ -168,6 +172,7 @@
     for load in loads:
         load.start()
     rx[...] = jnp.zeros_like(rx)
+    picked[...] = jnp.zeros_like(picked)
 
     my_y, my_x, my_c = gx // 16, (gx // 2) % 8, gx % 2
 
@@ -208,6 +213,7 @@
     to_last = (
         no, (gx == 1) & line0, no, (gx == 0) & (gy == 1) & (gz == 0), no, (gx == 0) & (gy == 0) & (gz == 1),
     )
+    slow = last | to_last[1] | to_last[3] | to_last[5]
     usual = (rank_at(gx + 1) > rank, rank_at(gx - 1) > rank, gy < 2, gy == 3, gz >= 0, no)
     later = [there[i] & (to_last[i] | (jnp.logical_not(last) & usual[i])) for i in range(6)]
     earlier = [there[i] & jnp.logical_not(later[i]) for i in range(6)]
@@ -246,8 +252,8 @@
 
     kpad[...] = jnp.zeros((LANES, LANES), F32)
     rpad[...] = jnp.zeros((8, LANES), F32)
-    loads[0].wait()
-    loads[1].wait()
+    for load in loads[:5]:
+        load.wait()
     kpad[0:NODES, 0:NODES] = stiff[...]
     rpad[0:1, 0:NODES] = relax[...]
     eye = iota((LANES, LANES), 0) == iota((LANES, LANES), 1)
@@ -262,16 +268,22 @@
     step4 = full(step2, step2)
     sum8 = sum4 + full(step4, sum4)
     elastic_op, acoustic_op = sum8 * (1.0 / 3.0), sum2
-    pl.when(jnp.logical_not(last))(answer_sides)
-
-    for load in loads[2:]:
+
+    for load in loads[5:]:
         load.wait()
     elastic = jnp.broadcast_to(mat[...], (LANES, COUNT)) > 0
     source = jnp.concatenate([src[0], src[1]], axis=1)
     field = jnp.where(elastic, full(elastic_op, source), full(acoustic_op, source))
     pick = face_rows()
-    high, low = halves(field)
-    faces = matmul(pick, high) + matmul(pick, low)
+    for t in range(2):
+        nodes[t, 0:LANES] = field[:, LANES * t : LANES * (t + 1)]
+        for f, (first, stride) in ((0, (0, 1)), (1, (100, 1)), (4, (0, 5)), (5, (4, 5))):
+            picked[t, FACE_ROWS * f : FACE_ROWS * f + FACE] = nodes[t, pl.ds(first, FACE, stride=stride)]
+        for f, first in ((2, 0), (3, 20)):
+            for a in range(5):
+                at = FACE_ROWS * f + 5 * a
+                picked[t, at : at + 5] = nodes[t, 25 * a + first : 25 * a + first + 5]
+    faces = jnp.concatenate([picked[0], picked[1]], axis=1)
     out = 2.0 * faces
     pack_halo(out, tx.at[0])
 
@@ -302,6 +314,8 @@
             @pl.when(there[i])
             def _():
                 halo_copy(step, i).wait_send()
+
+    pl.when(jnp.logical_not(last))(answer_sides)
 
     for i in range(6):
         halo_start(0, i, earlier[i])
@@ -413,7 +427,9 @@
         part = matmul_t(packer[k * LANES : (k + 1) * LANES], both)
         moved[k * LANES : (k + 1) * LANES] = part[:, 0:LANES] + part[:, LANES : 2 * LANES]
         for chunk in ORDER[8 * k : 8 * k + 8]:
-            pl.when(jnp.logical_not(line0 & (peer(chunk) == 0)))(lambda chunk=chunk: move(chunk).start())
+            held = line0 & (peer(chunk) == 0)
+            held = held if chunk // 4 == 1 else held | slow
+            pl.when(jnp.logical_not(held))(lambda chunk=chunk: move(chunk).start())
     landed[mine] = moved[SLOTS - CAP : SLOTS]
 
     change = on_traces(on_faces)
@@ -428,6 +444,11 @@
     for i in range(6):
         halo_start(1, i, there[i])
 
+    @pl.when(slow)
+    def _():
+        for chunk in LATE_ORDER:
+            pl.when(jnp.logical_not(line0 & (peer(chunk) == 0)))(lambda chunk=chunk: move(chunk).start())
+
     @pl.when(line0 & (gx > 0))
     def _():
         pl.semaphore_wait(first_sem, 1)
@@ -454,21 +475,18 @@
 
 def finish(landed, inc, settled_hbm, incoming_hbm, turned, out_sem):
     results = []
-    for f in range(6):
-        for t in range(2):
-            results.append(
-                pltpu.make_async_copy(
-                    inc.at[t, pl.ds(f * FACE_ROWS, FACE)],
-                    incoming_hbm.at[f, :, 0, pl.ds(t * LANES, LANES)],
-                    out_sem.at[2 * f + t],
-                )
-            )
-            results[-1].start()
     for k in range(4):
         turned[k] = landed[k * LANES : (k + 1) * LANES].T
         results.append(
             pltpu.make_async_copy(
-                turned.at[k, pl.ds(0, NODES)], settled_hbm.at[:, 0, pl.ds(k * LANES, LANES)], out_sem.at[12 + k]
+                turned.at[k, pl.ds(0, NODES)], settled_hbm.at[:, 0, pl.ds(k * LANES, LANES)], out_sem.at[2 + k]
+            )
+        )
+        results[-1].start()
+    for t in range(2):
+        results.append(
+            pltpu.make_async_copy(
+                inc.at[t, :, pl.ds(0, FACE)], incoming_hbm.at[:, :, 0, pl.ds(t * LANES, LANES)], out_sem.at[t]
             )
         )
         results[-1].start()
@@ -503,7 +521,7 @@
             pltpu.VMEM((SLOTS, LANES), F32),
             pltpu.VMEM((2, HALO_ROWS, LANES), F32),
             pltpu.VMEM((2, HALO_ROWS, LANES), F32),
-            pltpu.SemaphoreType.DMA((6,)),
+            pltpu.SemaphoreType.DMA((10,)),
             pltpu.SemaphoreType.DMA((2, 6)),
             pltpu.SemaphoreType.DMA((2, 6)),
             pltpu.SemaphoreType.DMA((GROUPS,)),
@@ -514,6 +532,8 @@
             pltpu.VMEM((16, LANES), F32),
             pltpu.SemaphoreType.DMA((2,)),
             pltpu.SemaphoreType.DMA((2,)),
+            pltpu.VMEM((2, LANES + 8, LANES), F32),
+            pltpu.VMEM((2, STACK, LANES), F32),
         ],
         compiler_params=pltpu.CompilerParams(
             collective_id=0, has_side_effects=True, vmem_limit_bytes=32 * 1024 * 1024
@@ -524,9 +544,9 @@
         out_shape=(pltpu.HBM((NODES, 1, SLOTS), F32), pltpu.HBM((6, FACE, 1, COUNT), F32)),
         in_specs=(vmem, vmem),
         out_specs=(anywhere, anywhere),
-        scratch_shapes=[pltpu.VMEM((4, LANES, LANES), F32), pltpu.SemaphoreType.DMA((16,))],
+        scratch_shapes=[pltpu.VMEM((4, LANES, LANES), F32), pltpu.SemaphoreType.DMA((6,))],
         compiler_params=pltpu.CompilerParams(vmem_limit_bytes=32 * 1024 * 1024),
-    )(landed, inc)
+    )(landed, inc.reshape(2, 6, FACE_ROWS, LANES))
     return (
         settled.reshape(1, 1, 1, NODES, SLOTS),
         incoming.reshape(1, 1, 1, 6, FACE, COUNT),

time: 24.7 us -> 24.2 us (0.980)
  Pallas kernels: 23.7 us -> 23.2 us
    pallas_call x1, Pallas kernels: 22.7 us -> 22.3 us  [shards(): pl.pallas_call(kernel, out_shape=(pltpu.VMEM((SLOTS, LANES), F32), pltpu....]
where the time goes in v4:
time: 24.2 us; the launch traced here: 23.9 us
  Pallas kernels  23.2 us (96%)
  between operations  0.64 us (3%)
    pallas_call x1, Pallas kernels, shards(): pl.pallas_call(kernel, out_shape=(pltpu.VMEM((SLOTS, LANES), F32), pltpu....  22.3 us
    pallas_call x1, Pallas kernels, shards(): pl.pallas_call(finish, out_shape=(pltpu.HBM((NODES, 1, SLOTS), F32), pltp...  0.9 us

profile of v4, /device:TPU:1, one launch (start us, length us, event | category | flops | bytes accessed | tf_op | source)
XLA Modules:
  0.0 23.9 jit_solution(186503372694620594)
XLA Ops:
  0.6 22.3 %shard_map.68 = (f32[512,128]{1,0:T(8,128)S(1)}, f32[2,192,128]{2,1,0:T(8,128)S(1)}) custom-call(f32[125,1,256]{2,1,0:T(1,128)} %bitcast.12, f32[125,125]{1,0:T(8,128)} %stiffness_hbm.1, f32[1,125]{1,0:T(1,128)} %bitcast.15, s32[1,256]{1,0:T(1,128)} %bitcast.13, s32[1,256]{1,0:T(1,128)} %bitcast.14), custom_call_target="tpu_custom_call" | custom-call | tf_op jit(solution)/shard_map/pallas_call | solution.py:507
  23.0 0.9 %shard_map.69 = (f32[125,1,512]{2,1,0:T(1,128)}, f32[6,25,1,256]{3,2,1,0:T(1,128)}) custom-call(f32[512,128]{1,0:T(8,128)S(1)} %get-tuple-element.6.landed, f32[2,6,32,128]{3,2,1,0:T(8,128)S(1)} %bitcast.11), custom_call_target="tpu_custom_call" | custom-call | tf_op jit(solution)/shard_map/pallas_call | solution.py:542

commit v5 on v4

--- a/solution.py
+++ b/solution.py
@@ -273,7 +273,8 @@
         load.wait()
     elastic = jnp.broadcast_to(mat[...], (LANES, COUNT)) > 0
     source = jnp.concatenate([src[0], src[1]], axis=1)
-    field = jnp.where(elastic, full(elastic_op, source), full(acoustic_op, source))
+    field = full(jnp.concatenate([elastic_op, acoustic_op], axis=0), source)
+    field = jnp.where(elastic, field[0:LANES], field[LANES : 2 * LANES])
     pick = face_rows()
     for t in range(2):
         nodes[t, 0:LANES] = field[:, LANES * t : LANES * (t + 1)]
@@ -292,7 +293,7 @@
         return pltpu.make_async_remote_copy(
             src_ref=tx.at[step, pl.ds(at, rows)],
             dst_ref=rx.at[step, pl.ds(at, rows)],
-            send_sem=halo_send.at[step, i],
+            send_sem=halo_send.at[i],
             recv_sem=halo_recv.at[step, i],
             device_id=sides[i],
             device_id_type=MESH,
@@ -317,7 +318,7 @@
 
     pl.when(jnp.logical_not(last))(answer_sides)
 
-    for i in range(6):
+    for i in (2, 3, 4, 5, 0, 1):
         halo_start(0, i, earlier[i])
 
     @pl.when(jnp.logical_not(last))
@@ -332,7 +333,7 @@
         return pltpu.make_async_remote_copy(
             src_ref=tx.at[0, pl.ds(at, rows)],
             dst_ref=relay.at[pl.ds(8 * k, rows)],
-            send_sem=halo_send.at[0, i],
+            send_sem=halo_send.at[i],
             recv_sem=relay_recv.at[k],
             device_id=(1, 0, 0),
             device_id_type=MESH,
@@ -413,8 +414,8 @@
         return pltpu.make_async_remote_copy(
             src_ref=moved.at[pl.ds(pl.multiple_of(chunk * CAP, CAP), CAP)],
             dst_ref=landed.at[mine],
-            send_sem=move_send.at[chunk],
-            recv_sem=move_recv.at[chunk],
+            send_sem=move_send.at[0],
+            recv_sem=move_recv.at[0],
             device_id=device or (peer(chunk), gy, gz),
             device_id_type=MESH,
         )
@@ -441,6 +442,7 @@
         @pl.when(to_last[i])
         def _():
             pl.semaphore_wait(side_sem.at[i], 1)
+    halo_wait_send(0)
     for i in range(6):
         halo_start(1, i, there[i])
 
@@ -459,9 +461,8 @@
     shift_inside(out, inc)
     halo_wait_recv(1)
     add_halo(rx.at[1], inc, there)
-    for chunk in ORDER:
-        move(chunk).wait_recv()
-    halo_wait_send(0)
+    chunks = landed.at[pl.ds(0, SLOTS - CAP)]
+    pltpu.make_async_copy(chunks, chunks, move_recv.at[0]).wait()
     halo_wait_send(1)
 
     @pl.when(to_last[1])
@@ -469,8 +470,8 @@
         for k, i in enumerate((3, 5)):
             relay_out(i, k).wait_send()
 
-    for chunk in ORDER:
-        move(chunk).wait_send()
+    chunks = moved.at[pl.ds(0, SLOTS - CAP)]
+    pltpu.make_async_copy(chunks, chunks, move_send.at[0]).wait()
 
 
 def finish(landed, inc, settled_hbm, incoming_hbm, turned, out_sem):
@@ -522,10 +523,10 @@
             pltpu.VMEM((2, HALO_ROWS, LANES), F32),
             pltpu.VMEM((2, HALO_ROWS, LANES), F32),
             pltpu.SemaphoreType.DMA((10,)),
+            pltpu.SemaphoreType.DMA((6,)),
             pltpu.SemaphoreType.DMA((2, 6)),
-            pltpu.SemaphoreType.DMA((2, 6)),
-            pltpu.SemaphoreType.DMA((GROUPS,)),
-            pltpu.SemaphoreType.DMA((GROUPS,)),
+            pltpu.SemaphoreType.DMA((1,)),
+            pltpu.SemaphoreType.DMA((1,)),
             pltpu.SemaphoreType.REGULAR((6,)),
             pltpu.SemaphoreType.REGULAR,
             pltpu.SemaphoreType.REGULAR,

time: 24.2 us -> 23.5 us (0.971)
  Pallas kernels: 23.2 us -> 22.6 us
    pallas_call x1, Pallas kernels: 22.3 us -> 21.7 us  [shards(): pl.pallas_call(kernel, out_shape=(pltpu.VMEM((SLOTS, LANES), F32), pltpu....]
where the time goes in v5:
time: 23.5 us; the launch traced here: 23.3 us
  Pallas kernels  22.6 us (96%)
  between operations  0.64 us (3%)
    pallas_call x1, Pallas kernels, shards(): pl.pallas_call(kernel, out_shape=(pltpu.VMEM((SLOTS, LANES), F32), pltpu....  21.7 us
    pallas_call x1, Pallas kernels, shards(): pl.pallas_call(finish, out_shape=(pltpu.HBM((NODES, 1, SLOTS), F32), pltp...  0.9 us

profile of v5, /device:TPU:1, one launch (start us, length us, event | category | flops | bytes accessed | tf_op | source)
XLA Modules:
  0.0 23.3 jit_solution(12651928426990517737)
XLA Ops:
  0.6 21.7 %shard_map.68 = (f32[512,128]{1,0:T(8,128)S(1)}, f32[2,192,128]{2,1,0:T(8,128)S(1)}) custom-call(f32[125,1,256]{2,1,0:T(1,128)} %bitcast.12, f32[125,125]{1,0:T(8,128)} %stiffness_hbm.1, f32[1,125]{1,0:T(1,128)} %bitcast.15, s32[1,256]{1,0:T(1,128)} %bitcast.13, s32[1,256]{1,0:T(1,128)} %bitcast.14), custom_call_target="tpu_custom_call" | custom-call | tf_op jit(solution)/shard_map/pallas_call | solution.py:508
  22.4 0.9 %shard_map.69 = (f32[125,1,512]{2,1,0:T(1,128)}, f32[6,25,1,256]{3,2,1,0:T(1,128)}) custom-call(f32[512,128]{1,0:T(8,128)S(1)} %get-tuple-element.6.landed, f32[2,6,32,128]{3,2,1,0:T(8,128)S(1)} %bitcast.11), custom_call_target="tpu_custom_call" | custom-call | tf_op jit(solution)/shard_map/pallas_call | solution.py:543

commit v6 on v5

--- a/solution.py
+++ b/solution.py
@@ -153,17 +153,17 @@
     source_hbm, stiffness_hbm, relax_hbm, owners_hbm, material_hbm,
     landed, inc,
     src, stiff, relax, owner, mat, kpad, rpad, packer, moved, tx, rx,
-    in_sem, halo_send, halo_recv, move_send, move_recv, side_sem, ready_sem, first_sem, relay, relay_send, relay_recv, nodes, picked,
+    in_sem, halo_send, halo_recv, move_send, move_recv, side_sem, ready_sem, first_sem, relay, nodes, picked,
 ):
     gx, gy, gz = (lax.axis_index(axis) for axis in ("gx", "gy", "gz"))
     loads = [
         *(
-            pltpu.make_async_copy(stiffness_hbm.at[pl.ds(at, rows)], stiff.at[pl.ds(at, rows)], in_sem.at[6 + k])
+            pltpu.make_async_copy(stiffness_hbm.at[pl.ds(at, rows)], stiff.at[pl.ds(at, rows)], in_sem.at[5 + k])
             for k, (at, rows) in enumerate(((0, 32), (32, 32), (64, 32), (96, 29)))
         ),
         pltpu.make_async_copy(relax_hbm, relax, in_sem.at[1]),
         pltpu.make_async_copy(source_hbm.at[:, 0, pl.ds(0, LANES)], src.at[0, pl.ds(0, NODES)], in_sem.at[2]),
-        pltpu.make_async_copy(source_hbm.at[:, 0, pl.ds(LANES, LANES)], src.at[1, pl.ds(0, NODES)], in_sem.at[5]),
+        pltpu.make_async_copy(source_hbm.at[:, 0, pl.ds(LANES, LANES)], src.at[1, pl.ds(0, NODES)], in_sem.at[0]),
         pltpu.make_async_copy(owners_hbm, owner, in_sem.at[3]),
         pltpu.make_async_copy(material_hbm, mat, in_sem.at[4]),
     ]
@@ -334,7 +334,7 @@
             src_ref=tx.at[0, pl.ds(at, rows)],
             dst_ref=relay.at[pl.ds(8 * k, rows)],
             send_sem=halo_send.at[i],
-            recv_sem=relay_recv.at[k],
+            recv_sem=halo_recv.at[0, i - 1],
             device_id=(1, 0, 0),
             device_id_type=MESH,
         )
@@ -344,7 +344,7 @@
         return pltpu.make_async_remote_copy(
             src_ref=relay.at[pl.ds(8 * k, rows)],
             dst_ref=rx.at[0, pl.ds(at, rows)],
-            send_sem=relay_send.at[k],
+            send_sem=halo_send.at[i],
             recv_sem=halo_recv.at[0, i],
             device_id=(0, 0, 0),
             device_id_type=MESH,
@@ -522,7 +522,7 @@
             pltpu.VMEM((SLOTS, LANES), F32),
             pltpu.VMEM((2, HALO_ROWS, LANES), F32),
             pltpu.VMEM((2, HALO_ROWS, LANES), F32),
-            pltpu.SemaphoreType.DMA((10,)),
+            pltpu.SemaphoreType.DMA((9,)),
             pltpu.SemaphoreType.DMA((6,)),
             pltpu.SemaphoreType.DMA((2, 6)),
             pltpu.SemaphoreType.DMA((1,)),
@@ -531,8 +531,6 @@
             pltpu.SemaphoreType.REGULAR,
             pltpu.SemaphoreType.REGULAR,
             pltpu.VMEM((16, LANES), F32),
-            pltpu.SemaphoreType.DMA((2,)),
-            pltpu.SemaphoreType.DMA((2,)),
             pltpu.VMEM((2, LANES + 8, LANES), F32),
             pltpu.VMEM((2, STACK, LANES), F32),
         ],

time: 23.5 us -> 23.5 us (level)
  no operation moved by 1% of the time
where the time goes in v6:
time: 23.5 us; the launch traced here: 23.2 us
  Pallas kernels  22.6 us (96%)
  between operations  0.64 us (3%)
    pallas_call x1, Pallas kernels, shards(): pl.pallas_call(kernel, out_shape=(pltpu.VMEM((SLOTS, LANES), F32), pltpu....  21.7 us
    pallas_call x1, Pallas kernels, shards(): pl.pallas_call(finish, out_shape=(pltpu.HBM((NODES, 1, SLOTS), F32), pltp...  0.9 us

profile of v6, /device:TPU:1, one launch (start us, length us, event | category | flops | bytes accessed | tf_op | source)
XLA Modules:
  0.0 23.2 jit_solution(5842100504638386698)
XLA Ops:
  0.6 21.7 %shard_map.68 = (f32[512,128]{1,0:T(8,128)S(1)}, f32[2,192,128]{2,1,0:T(8,128)S(1)}) custom-call(f32[125,1,256]{2,1,0:T(1,128)} %bitcast.12, f32[125,125]{1,0:T(8,128)} %stiffness_hbm.1, f32[1,125]{1,0:T(1,128)} %bitcast.15, s32[1,256]{1,0:T(1,128)} %bitcast.13, s32[1,256]{1,0:T(1,128)} %bitcast.14), custom_call_target="tpu_custom_call" | custom-call | tf_op jit(solution)/shard_map/pallas_call | solution.py:508
  22.3 0.9 %shard_map.69 = (f32[125,1,512]{2,1,0:T(1,128)}, f32[6,25,1,256]{3,2,1,0:T(1,128)}) custom-call(f32[512,128]{1,0:T(8,128)S(1)} %get-tuple-element.6.landed, f32[2,6,32,128]{3,2,1,0:T(8,128)S(1)} %bitcast.11), custom_call_target="tpu_custom_call" | custom-call | tf_op jit(solution)/shard_map/pallas_call | solution.py:541
